TPU v7x, 512 devices: a whole 4x8x8 slice. The times are simulated.
512 devices in a mesh: seq: 128 (over y_hi, x, z, core), head: 4 (over y_lo).
Axes of the slice: x: 4, y: 8 (y_hi: 2, y_lo: 4; y = y_hi * 4 + y_lo), z: 8, core: 2. Of those that a mesh axis runs over, the one named last changes fastest.
Arguments:
- shared_qk: bfloat16 [65536, 512], P('seq', 'head'), may hold values from -300 to 300
- value_rows: bfloat16 [65536, 512], P('seq', 'head'), may hold values from -12 to 12
- out_grad: bfloat16 [65536, 512], P('seq', 'head'), may hold values from -6 to 6
- bucket_order: int32 [4, 65536], P('head', 'seq'), may hold values from 0 to 65535, as said below
- inverse_order: int32 [4, 65536], P('head', 'seq'), may hold values from 0 to 65535, as said below
Outputs:
- attended: bfloat16 [65536, 512], P('seq', 'head')
- grad_qk: bfloat16 [65536, 512], P('seq', 'head')
- grad_v: bfloat16 [65536, 512], P('seq', 'head')
Inputs may be any that keep to these rules, and one draw needn't show every extreme that they name: `bucket_order`: each row is a permutation of the positions. Cut positions and slots into aligned blocks of 512: for every group and every pair of a position block and a slot block, at most 6 positions of the one have slots in the other, and 6 is reached in every group by some pair for every slot block and every position block. inverse_order[g, bucket_order[g, s]] = s.
All inputs are finite; a program needn't handle non-finite values.
Results may differ from a plain program's by a relative error of at most 0.025.
Values may be sent and summed in bfloat16 or wider, within the bound.
No kernel may reach another device: no remote copies, remote signals or barrier semaphores. Data moves between devices by JAX's collectives and lax.ppermute only.
A program may use at most 64 MiB of HBM per device.

v0:
```python
import jax
import jax.numpy as jnp
from jax import lax
from jax.sharding import PartitionSpec as P

HEAD_DIM = 64
BLOCK = 512


self_score = -100000.0
masked_score = -1000000000.0
norm_eps = 1e-06


def from_behind(block, axis, distance):
    devices = range(lax.axis_size(axis))
    route = [((i - distance) % len(devices), i) for i in devices]
    return lax.ppermute(block, axis, route)


def head_weights(query_rows, key_rows, inverse_norm, query_pos, key_pos):
    dots = jnp.dot(query_rows, key_rows.T, preferred_element_type=jnp.float32)
    raw_score = dots * inverse_norm[None, :]
    earlier = key_pos[None, :] < query_pos[:, None]
    itself = key_pos[None, :] == query_pos[:, None]
    score = jnp.where(
        earlier, raw_score, jnp.where(itself, jnp.float32(self_score), jnp.float32(masked_score))
    )
    top_score = jnp.max(score, axis=1, keepdims=True)
    expo = jnp.exp(score - top_score)
    weights = expo / jnp.sum(expo, axis=1, keepdims=True)
    return (raw_score, weights)


def head_output(weights, value_keys):
    weight_bf = weights.astype(jnp.bfloat16)
    output_rows = jnp.dot(weight_bf, value_keys, preferred_element_type=jnp.float32).astype(
        jnp.bfloat16
    )
    return (weight_bf, output_rows)


def head_grads(
    raw_score,
    weights,
    weight_bf,
    query_rows,
    key_rows,
    value_keys,
    inverse_norm,
    grad_rows,
    output_rows,
):
    value_dots = jnp.dot(grad_rows, value_keys.T, preferred_element_type=jnp.float32)
    row_delta = jnp.sum(
        grad_rows.astype(jnp.float32) * output_rows.astype(jnp.float32), axis=1, keepdims=True
    )
    dscore = weights * (value_dots - row_delta)
    score_grad = (dscore * inverse_norm[None, :]).astype(jnp.bfloat16)
    query_grad = jnp.dot(score_grad, key_rows, preferred_element_type=jnp.float32)
    scaled_sum = jnp.sum(dscore * raw_score, axis=0)
    key_grad = jnp.dot(score_grad.T, query_rows, preferred_element_type=jnp.float32)
    key_grad = key_grad - (scaled_sum * inverse_norm * inverse_norm)[:, None] * key_rows.astype(
        jnp.float32
    )
    value_grad = jnp.dot(weight_bf.T, grad_rows, preferred_element_type=jnp.float32)
    return (query_grad, key_grad, value_grad)


def per_device(shared_qk, value_rows, out_grad, bucket_order, inverse_order):
    peer_count = lax.axis_size("seq")
    local_rows = shared_qk.shape[0]
    group_width = shared_qk.shape[1]
    heads_here = group_width // HEAD_DIM
    capacity = 3 * local_rows // (2 * peer_count)
    positions = bucket_order[0]
    slot_of = inverse_order[0]
    target = slot_of // local_rows
    local_slot = slot_of % local_rows
    onehot = (target[:, None] == jnp.arange(peer_count, dtype=jnp.int32)[None, :]).astype(jnp.int32)
    order_within = jnp.sum((jnp.cumsum(onehot, axis=0) - onehot) * onehot, axis=1)
    buffer_slot = target * capacity + order_within
    source_row = (
        jnp.full((peer_count * capacity,), local_rows, jnp.int32)
        .at[buffer_slot]
        .set(jnp.arange(local_rows, dtype=jnp.int32))
    )
    sent_slot = jnp.concatenate([local_slot, jnp.full((1,), local_rows, jnp.int32)])[source_row]
    sent_slot = sent_slot.reshape(peer_count, capacity)

    def pack_rows(rows_in):
        padded = jnp.concatenate([rows_in, jnp.zeros((1, rows_in.shape[1]), rows_in.dtype)], axis=0)
        return padded[source_row].reshape(peer_count, capacity, rows_in.shape[1])

    def unpack_rows(arrived, arrival_flat):
        width_in = arrived.shape[2]
        flat_rows = arrived.reshape(peer_count * capacity, width_in)
        padded = jnp.concatenate([flat_rows, jnp.zeros((1, width_in), arrived.dtype)], axis=0)
        where_from = (
            jnp.full((local_rows + 1,), peer_count * capacity, jnp.int32)
            .at[arrival_flat]
            .set(jnp.arange(peer_count * capacity, dtype=jnp.int32))
        )
        return padded[where_from[:local_rows]]

    def return_rows(sorted_in, arrival_flat):
        padded = jnp.concatenate(
            [sorted_in, jnp.zeros((1, sorted_in.shape[1]), sorted_in.dtype)], axis=0
        )
        return padded[arrival_flat].reshape(peer_count, capacity, sorted_in.shape[1])

    def restore_rows(returned):
        return returned.reshape(peer_count * capacity, returned.shape[2])[buffer_slot]

    joined = jnp.concatenate([shared_qk, value_rows], axis=1)
    arrived, arrival = (
        lax.all_to_all(pack_rows(joined), "seq", split_axis=0, concat_axis=0, tiled=True),
        lax.all_to_all(sent_slot, "seq", split_axis=0, concat_axis=0, tiled=True),
    )
    arrival_flat = arrival.reshape(-1)
    sorted_rows = unpack_rows(arrived, arrival_flat)
    sorted_q = sorted_rows[:, :group_width]
    sorted_v = sorted_rows[:, group_width : 2 * group_width]
    prior_rows, prior_pos = from_behind((sorted_rows, positions), "seq", 1)
    key_q_all = jnp.concatenate([prior_rows[:, :group_width], sorted_q], axis=0)
    key_v_all = jnp.concatenate([prior_rows[:, group_width:], sorted_v], axis=0)
    key_pos_all = jnp.concatenate([prior_pos, positions], axis=0)
    key_float = key_q_all.astype(jnp.float32).reshape(BLOCK + local_rows, heads_here, HEAD_DIM)
    norm_all = lax.rsqrt(jnp.sum(key_float * key_float, axis=2) + norm_eps)

    def block_inputs(block_at, head_at):
        first_row = block_at * BLOCK
        first_col = head_at * HEAD_DIM
        query_rows = sorted_q[first_row : first_row + BLOCK, first_col : first_col + HEAD_DIM]
        key_rows = key_q_all[first_row : first_row + 2 * BLOCK, first_col : first_col + HEAD_DIM]
        value_keys = key_v_all[first_row : first_row + 2 * BLOCK, first_col : first_col + HEAD_DIM]
        inverse_norm = norm_all[first_row : first_row + 2 * BLOCK, head_at]
        return (query_rows, key_rows, value_keys, inverse_norm, positions, key_pos_all)

    key_acc = jnp.zeros((BLOCK + local_rows, group_width), jnp.float32)
    value_acc = jnp.zeros((BLOCK + local_rows, group_width), jnp.float32)
    block_at = 0
    out_heads = []
    for head_at in range(heads_here):
        query_rows, key_rows, value_keys, inverse_norm, query_pos, key_pos = block_inputs(
            block_at, head_at
        )
        raw_score, weights = head_weights(query_rows, key_rows, inverse_norm, query_pos, key_pos)
        weight_bf, output_rows = head_output(weights, value_keys)
        out_heads.append(output_rows)
    out_blocks = jnp.concatenate(out_heads, axis=1)
    returned = lax.all_to_all(
        return_rows(out_blocks, arrival_flat), "seq", split_axis=0, concat_axis=0, tiled=True
    )
    attended = restore_rows(returned)
    grad_arrived = lax.all_to_all(
        pack_rows(out_grad), "seq", split_axis=0, concat_axis=0, tiled=True
    )
    sorted_g = unpack_rows(grad_arrived, arrival_flat)
    block_at = 0
    query_heads = []
    for head_at in range(heads_here):
        query_rows, key_rows, value_keys, inverse_norm, query_pos, key_pos = block_inputs(
            block_at, head_at
        )
        first_row = block_at * BLOCK
        first_col = head_at * HEAD_DIM
        grad_rows = sorted_g[first_row : first_row + BLOCK, first_col : first_col + HEAD_DIM]
        output_rows = out_blocks[first_row : first_row + BLOCK, first_col : first_col + HEAD_DIM]
        raw_score, weights = head_weights(query_rows, key_rows, inverse_norm, query_pos, key_pos)
        weight_bf = weights.astype(jnp.bfloat16)
        query_grad, key_grad, value_grad = head_grads(
            raw_score,
            weights,
            weight_bf,
            query_rows,
            key_rows,
            value_keys,
            inverse_norm,
            grad_rows,
            output_rows,
        )
        query_heads.append(query_grad)
        key_acc = key_acc.at[
            first_row : first_row + 2 * BLOCK, first_col : first_col + HEAD_DIM
        ].add(key_grad)
        value_acc = value_acc.at[
            first_row : first_row + 2 * BLOCK, first_col : first_col + HEAD_DIM
        ].add(value_grad)
    query_blocks = jnp.concatenate(query_heads, axis=1)
    outgoing = jnp.concatenate([key_acc[:BLOCK], value_acc[:BLOCK]], axis=1)
    incoming = from_behind(outgoing.astype(jnp.bfloat16), "seq", -1).astype(outgoing.dtype)
    key_local = key_acc[BLOCK:].at[local_rows - BLOCK :].add(incoming[:, :group_width])
    value_local = value_acc[BLOCK:].at[local_rows - BLOCK :].add(incoming[:, group_width:])
    grad_q_sorted = (query_blocks + key_local).astype(jnp.bfloat16)
    grad_v_sorted = value_local.astype(jnp.bfloat16)
    results = jnp.concatenate([grad_q_sorted, grad_v_sorted], axis=1)
    returned = lax.all_to_all(
        return_rows(results, arrival_flat), "seq", split_axis=0, concat_axis=0, tiled=True
    )
    restored = restore_rows(returned)
    grad_qk = restored[:, :group_width]
    grad_v = restored[:, group_width:]
    return (attended, grad_qk, grad_v)


def solution(mesh):
    placed = (
        P("seq", "head"),
        P("seq", "head"),
        P("seq", "head"),
        P("head", "seq"),
        P("head", "seq"),
    )
    return jax.shard_map(
        per_device,
        mesh=mesh,
        in_specs=placed,
        out_specs=(P("seq", "head"), P("seq", "head"), P("seq", "head")),
        check_vma=False,
    )
```

profile of v0, /device:TPU:1, one launch (start us, length us, event | category | flops | bytes accessed | tf_op | source)
XLA Modules:
  0.0 200.2 jit_solution(8404132071272995504)
XLA Ops:
  0.6 0.7 add_select_fusion.1
  1.3 0.7 add_select_fusion
  2.7 0.7 compare_select_fusion.1
  3.4 0.6 copy-done.9
  4.0 2.4 %scatter_custom_fusion = s32[768]{0:T(1024)S(1)} fusion(s32[512]{0:T(512)S(1)} %bitcast.68, s32[512]{0:T(512)S(1)} %iota.19, s32[]{:T(128)} %constant.206.clone.1), kind=kCustom, calls=%fused_computation.121 | custom fusion | bytes 3076 | tf_op jit(solution)/shard_map/scatter | solution.py:86
  6.5 3.2 %gather_fusion.1 = s32[768]{0:T(1024)S(1)} fusion(s32[513]{0:T(1024)S(1)} %pad_add_fusion.1, s32[1024]{0:T(1024)S(1)} %pad_clamp_fusion.3), kind=kCustom, calls=%fused_computation.1 | custom fusion | bytes 9216 | tf_op jit(solution)/shard_map/gather | solution.py:88
  9.7 0.8 all_to_all.19
  10.4 20.9 %all-to-all-start.1 = ((s32[128,1,6]{2,1,0:T(1,128)}), s32[128,1,6]{2,1,0:T(1,128)S(1)}, u32[]{:S(2)}, u32[]{:S(2)}) async-start(s32[128,1,6]{2,1,0:T(1,128)} %bitcast.9), calls=%async_computation.1 | async-start | bytes 131072 | tf_op jit(solution)/shard_map/all_to_all | solution.py:118
  31.4 1.9 gather_fusion.5
  33.2 0.8 reshape.350
  34.0 11.7 %all-to-all-done.1 = s32[128,1,6]{2,1,0:T(1,128)S(1)} async-done(((s32[128,1,6]{2,1,0:T(1,128)}), s32[128,1,6]{2,1,0:T(1,128)S(1)}, u32[]{:S(2)}, u32[]{:S(2)}) %all-to-all-start.1) | async-done | bytes 3104 | tf_op jit(solution)/shard_map/all_to_all | solution.py:118
  45.7 5.8 %all-to-all-start.3 = ((bf16[128,6,128]{2,1,0:T(8,128)(2,1)}), bf16[128,6,128]{2,1,0:T(8,128)(2,1)S(1)}, u32[]{:S(2)}, u32[]{:S(2)}) async-start(bf16[128,6,128]{2,1,0:T(8,128)(2,1)} %reshape.350), calls=%async_computation.3 | async-start | bytes 524288 | tf_op jit(solution)/shard_map/all_to_all | solution.py:156
  51.5 2.7 %gather_fusion = bf16[768,256]{1,0:T(8,128)(2,1)S(1)} fusion(bf16[513,256]{1,0:T(8,128)(2,1)S(1)} %fusion.15, s32[1024]{0:T(1024)S(1)} %pad_clamp_fusion.3), kind=kCustom, calls=%fused_computation | custom fusion | bytes 789504 | tf_op jit(solution)/shard_map/gather | solution.py:93
  54.2 0.9 reshape.345
  55.1 12.3 %all-to-all-done.3 = bf16[128,6,128]{2,1,0:T(8,128)(2,1)S(1)} async-done(((bf16[128,6,128]{2,1,0:T(8,128)(2,1)}), bf16[128,6,128]{2,1,0:T(8,128)(2,1)S(1)}, u32[]{:S(2)}, u32[]{:S(2)}) %all-to-all-start.3) | async-done | bytes 196640 | tf_op jit(solution)/shard_map/all_to_all | solution.py:156
  67.4 7.4 %all-to-all-start = ((bf16[128,6,256]{2,1,0:T(8,128)(2,1)}), bf16[128,6,256]{2,1,0:T(8,128)(2,1)S(1)}, u32[]{:S(2)}, u32[]{:S(2)}) async-start(bf16[128,6,256]{2,1,0:T(8,128)(2,1)} %reshape.345), calls=%async_computation | async-start | bytes 1048576 | tf_op jit(solution)/shard_map/all_to_all | solution.py:117
  74.8 3.5 %collective-permute-start = (s32[512]{0:T(512)S(1)}, s32[512]{0:T(512)S(1)}, u32[]{:S(2)}, u32[]{:S(2)}) collective-permute-start(s32[512]{0:T(512)S(1)} %bitcast.55), channel_id=1, source_target_pairs={{508,0},{0,4},{4,8},{8,12},{12,16},{16,20},{20,24},{24,28},{28,32}... | collective-permute-start | bytes 6152 | tf_op jit(solution)/shard_map/ppermute | solution.py:18
  78.4 0.6 compare_reduce_fusion
  79.1 0.5 broadcast.359
  79.6 0.8 reduce.25
  80.6 3.6 %scatter_custom_fusion.1 = s32[513]{0:T(1024)S(1)} fusion(s32[768]{0:T(1024)S(1)} %fusion.39, s32[768]{0:T(1024)S(1)} %iota.20, s32[]{:T(128)} %constant.213.clone.1), kind=kCustom, calls=%fused_computation.117 | custom fusion | bytes 2056 | tf_op jit(solution)/shard_map/scatter | solution.py:102
  84.3 1.3 gather_fusion.6
  85.7 9.9 %all-to-all-done = bf16[128,6,256]{2,1,0:T(8,128)(2,1)S(1)} async-done(((bf16[128,6,256]{2,1,0:T(8,128)(2,1)}), bf16[128,6,256]{2,1,0:T(8,128)(2,1)S(1)}, u32[]{:S(2)}, u32[]{:S(2)}) %all-to-all-start) | async-done | bytes 393248 | tf_op jit(solution)/shard_map/all_to_all | solution.py:117
  95.7 2.0 gather_fusion.2
  97.8 4.3 %collective-permute-start.1 = (bf16[512,256]{0,1:T(8,128)(2,1)S(1)}, bf16[512,256]{0,1:T(8,128)(2,1)S(1)}, u32[]{:S(2)}, u32[]{:S(2)}) collective-permute-start(bf16[512,256]{0,1:T(8,128)(2,1)S(1)} %copy.28), channel_id=1, source_target_pairs={{508,0},{0,4},{4,8},{8,12},{12,16},{16,20},{20,24},{24,28},{28,32}... | collective-permute-start | bytes 786440 | tf_op jit(solution)/shard_map/ppermute | solution.py:18
  102.5 2.9 %collective-permute-done.1 = bf16[512,256]{0,1:T(8,128)(2,1)S(1)} collective-permute-done((bf16[512,256]{0,1:T(8,128)(2,1)S(1)}, bf16[512,256]{0,1:T(8,128)(2,1)S(1)}, u32[]{:S(2)}, u32[]{:S(2)}) %collective-permute-start.1) | collective-permute-done | bytes 262176 | tf_op jit(solution)/shard_map/ppermute | solution.py:18
  105.5 0.5 fusion.32
  106.1 0.9 fusion.55
  107.0 1.3 fusion.1
  108.3 1.3 fusion
  110.1 1.2 multiply_reduce_fusion.1
  111.2 0.9 convolution_select_fusion
  113.0 2.6 %multiply_reduce_fusion = (f32[1024]{0:T(1024)}, f32[512,1024]{1,0:T(8,128)}) fusion(f32[512,1024]{1,0:T(8,128)S(1)} %fusion.32, f32[1024]{0:T(1024)S(1)} %bitcast.52, f32[512,1024]{1,0:T(8,128)S(1)} %get-tuple-element.110, f32[512]{0:T(512)S(1)} %get-tuple-element.118, bf16[512,128]{0,1:T(8,128)(2,1)S(1)} %get-tuple-element.101, ...), kind=kOutput, calls=%fused_computation.13 | convolution fusion | flops 69991424 | bytes 6694912 | tf_op jit(solution)/shard_map/dot_general | solution.py:54
  115.8 2.5 %gather_fusion.3 = bf16[768,128]{1,0:T(8,128)(2,1)} fusion(bf16[513,128]{1,0:T(8,128)(2,1)S(1)} %concatenate.80.clone, s32[1024]{0:T(1024)S(1)} %pad_clamp_fusion.1), kind=kCustom, calls=%fused_computation.3 | custom fusion | bytes 396288 | tf_op jit(solution)/shard_map/gather | solution.py:110
  118.3 1.7 reshape.348
  120.0 16.8 %all-to-all-start.2 = ((bf16[128,6,128]{2,1,0:T(8,128)(2,1)}), bf16[128,6,128]{2,1,0:T(8,128)(2,1)S(1)}, u32[]{:S(2)}, u32[]{:S(2)}) async-start(bf16[128,6,128]{2,1,0:T(8,128)(2,1)} %reshape.348), calls=%async_computation.2 | async-start | bytes 524288 | tf_op jit(solution)/shard_map/all_to_all | solution.py:152
  136.8 2.2 %fusion.14 = f32[512,64]{0,1:T(8,128)S(1)} fusion(f32[512,1024]{1,0:T(8,128)} %get-tuple-element.121, f32[1024]{0:T(1024)S(1)} %bitcast.53, bf16[512,128]{0,1:T(8,128)(2,1)S(1)} %get-tuple-element.102, bf16[512,128]{0,1:T(8,128)(2,1)S(1)} %get-tuple-element.100), kind=kOutput, calls=%fused_computation.45 | convolution fusion | flops 68419584 | bytes 2494464 | tf_op jit(solution)/shard_map/dot_general | solution.py:60
  139.0 0.7 multiply_multiply_fusion.1
  140.2 0.9 fusion.4
  141.2 2.9 %collective-permute-start.2 = (bf16[512,256]{0,1:T(8,128)(2,1)S(1)}, bf16[512,256]{0,1:T(8,128)(2,1)S(1)}, u32[]{:S(2)}, u32[]{:S(2)}) collective-permute-start(bf16[512,256]{0,1:T(8,128)(2,1)S(1)} %pad_maximum_fusion.2), channel_id=1, source_target_pairs={{4,0},{8,4},{12,8},{16,12},{20,16},{24,20},{28,24},{32,28},{36,32}... | collective-permute-start | bytes 786440 | tf_op jit(solution)/shard_map/ppermute | solution.py:18
  144.5 5.8 %collective-permute-done.2 = bf16[512,256]{0,1:T(8,128)(2,1)S(1)} collective-permute-done((bf16[512,256]{0,1:T(8,128)(2,1)S(1)}, bf16[512,256]{0,1:T(8,128)(2,1)S(1)}, u32[]{:S(2)}, u32[]{:S(2)}) %collective-permute-start.2) | collective-permute-done | bytes 262176 | tf_op jit(solution)/shard_map/ppermute | solution.py:18
  150.7 2.7 %gather_fusion.7 = bf16[768,256]{1,0:T(8,128)(2,1)S(1)} fusion(bf16[513,256]{1,0:T(8,128)(2,1)S(1)} %concatenate.86.clone, s32[1024]{0:T(1024)S(1)} %copy-done.7), kind=kCustom, calls=%fused_computation.7 | custom fusion | bytes 789504 | tf_op jit(solution)/shard_map/gather | solution.py:110
  153.4 0.9 reshape.352
  154.3 20.3 %all-to-all-start.4 = ((bf16[128,6,256]{2,1,0:T(8,128)(2,1)}), bf16[128,6,256]{2,1,0:T(8,128)(2,1)S(1)}, u32[]{:S(2)}, u32[]{:S(2)}) async-start(bf16[128,6,256]{2,1,0:T(8,128)(2,1)} %reshape.352), calls=%async_computation.4 | async-start | bytes 1048576 | tf_op jit(solution)/shard_map/all_to_all | solution.py:198
  174.7 1.9 gather_fusion.4
  176.6 20.8 %all-to-all-done.4 = bf16[128,6,256]{2,1,0:T(8,128)(2,1)S(1)} async-done(((bf16[128,6,256]{2,1,0:T(8,128)(2,1)}), bf16[128,6,256]{2,1,0:T(8,128)(2,1)S(1)}, u32[]{:S(2)}, u32[]{:S(2)}) %all-to-all-start.4) | async-done | bytes 393248 | tf_op jit(solution)/shard_map/all_to_all | solution.py:198
  197.5 2.0 gather_fusion.8
  199.5 0.7 fusion.59
  (76 shorter events, 4.8 us)
Async XLA Ops:
  3.4 0.6 copy-start.9
  6.4 24.9 %copy-start.1 = (bf16[512,128]{1,0:T(8,128)(2,1)S(1)}, bf16[512,128]{1,0:T(8,128)(2,1)}, u32[]{:S(2)}) copy-start(bf16[512,128]{1,0:T(8,128)(2,1)} %param.23) | copy-start | bytes 393220
  9.7 41.8 %copy-start.2 = (bf16[512,128]{1,0:T(8,128)(2,1)S(1)}, bf16[512,128]{1,0:T(8,128)(2,1)}, u32[]{:S(2)}) copy-start(bf16[512,128]{1,0:T(8,128)(2,1)} %param.22) | copy-start | bytes 393220
  9.7 41.8 %copy-start.3 = (bf16[512,128]{1,0:T(8,128)(2,1)S(1)}, bf16[512,128]{1,0:T(8,128)(2,1)}, u32[]{:S(2)}) copy-start(bf16[512,128]{1,0:T(8,128)(2,1)} %param.21) | copy-start | bytes 393220
  10.4 35.2 %all-to-all-start.1 = ((s32[128,1,6]{2,1,0:T(1,128)}), s32[128,1,6]{2,1,0:T(1,128)S(1)}, u32[]{:S(2)}, u32[]{:S(2)}) async-start(s32[128,1,6]{2,1,0:T(1,128)} %bitcast.9), calls=%async_computation.1 | async-start | bytes 131072 | tf_op jit(solution)/shard_map/all_to_all | solution.py:118
  45.7 21.7 %all-to-all-start.3 = ((bf16[128,6,128]{2,1,0:T(8,128)(2,1)}), bf16[128,6,128]{2,1,0:T(8,128)(2,1)S(1)}, u32[]{:S(2)}, u32[]{:S(2)}) async-start(bf16[128,6,128]{2,1,0:T(8,128)(2,1)} %reshape.350), calls=%async_computation.3 | async-start | bytes 524288 | tf_op jit(solution)/shard_map/all_to_all | solution.py:156
  51.5 23.3 %copy-start.8 = (s32[1,512]{1,0:T(1,128)S(1)}, s32[1,512]{1,0:T(1,128)}, u32[]{:S(2)}) copy-start(s32[1,512]{1,0:T(1,128)} %param.24) | copy-start | bytes 6148
  67.4 28.1 %all-to-all-start = ((bf16[128,6,256]{2,1,0:T(8,128)(2,1)}), bf16[128,6,256]{2,1,0:T(8,128)(2,1)S(1)}, u32[]{:S(2)}, u32[]{:S(2)}) async-start(bf16[128,6,256]{2,1,0:T(8,128)(2,1)} %reshape.345), calls=%async_computation | async-start | bytes 1048576 | tf_op jit(solution)/shard_map/all_to_all | solution.py:117
  74.8 4.3 %collective-permute-start = (s32[512]{0:T(512)S(1)}, s32[512]{0:T(512)S(1)}, u32[]{:S(2)}, u32[]{:S(2)}) collective-permute-start(s32[512]{0:T(512)S(1)} %bitcast.55), channel_id=1, source_target_pairs={{508,0},{0,4},{4,8},{8,12},{12,16},{16,20},{20,24},{24,28},{28,32}... | collective-permute-start | bytes 6152 | tf_op jit(solution)/shard_map/ppermute | solution.py:18
  84.2 31.6 %copy-start.6 = (s32[1024]{0:T(1024)}, s32[1024]{0:T(1024)S(1)}, u32[]{:S(2)}) copy-start(s32[1024]{0:T(1024)S(1)} %pad_clamp_fusion.1) | copy-start | bytes 12292
  97.8 7.6 %collective-permute-start.1 = (bf16[512,256]{0,1:T(8,128)(2,1)S(1)}, bf16[512,256]{0,1:T(8,128)(2,1)S(1)}, u32[]{:S(2)}, u32[]{:S(2)}) collective-permute-start(bf16[512,256]{0,1:T(8,128)(2,1)S(1)} %copy.28), channel_id=1, source_target_pairs={{508,0},{0,4},{4,8},{8,12},{12,16},{16,20},{20,24},{24,28},{28,32}... | collective-permute-start | bytes 786440 | tf_op jit(solution)/shard_map/ppermute | solution.py:18
  106.0 1.0 copy-start.4
  118.3 20.7 %copy-start.5 = (f32[1024,2]{0,1:T(2,128)S(1)}, f32[1024,2]{0,1:T(2,128)}, u32[]{:S(2)}) copy-start(f32[1024,2]{0,1:T(2,128)} %copy-done.4) | copy-start | bytes 24580
  120.0 34.3 %all-to-all-start.2 = ((bf16[128,6,128]{2,1,0:T(8,128)(2,1)}), bf16[128,6,128]{2,1,0:T(8,128)(2,1)S(1)}, u32[]{:S(2)}, u32[]{:S(2)}) async-start(bf16[128,6,128]{2,1,0:T(8,128)(2,1)} %reshape.348), calls=%async_computation.2 | async-start | bytes 524288 | tf_op jit(solution)/shard_map/all_to_all | solution.py:152
  136.8 2.9 %copy-start = (f32[512,1024]{1,0:T(8,128)S(1)}, f32[512,1024]{1,0:T(8,128)}, u32[]{:S(2)}) copy-start(f32[512,1024]{1,0:T(8,128)} %get-tuple-element.121) | copy-start | bytes 6291460
  141.2 9.2 %collective-permute-start.2 = (bf16[512,256]{0,1:T(8,128)(2,1)S(1)}, bf16[512,256]{0,1:T(8,128)(2,1)S(1)}, u32[]{:S(2)}, u32[]{:S(2)}) collective-permute-start(bf16[512,256]{0,1:T(8,128)(2,1)S(1)} %pad_maximum_fusion.2), channel_id=1, source_target_pairs={{4,0},{8,4},{12,8},{16,12},{20,16},{24,20},{28,24},{32,28},{36,32}... | collective-permute-start | bytes 786440 | tf_op jit(solution)/shard_map/ppermute | solution.py:18
  144.5 6.2 %copy-start.7 = (s32[1024]{0:T(1024)S(1)}, s32[1024]{0:T(1024)}, u32[]{:S(2)}) copy-start(s32[1024]{0:T(1024)} %copy-done.6) | copy-start | bytes 12292
  150.7 23.9 %copy-start.10 = (s32[512,1]{0,1:T(1,128)S(1)}, s32[512,1]{0,1:T(1,128)}, u32[]{:S(2)}) copy-start(s32[512,1]{0,1:T(1,128)} %copy-done.9) | copy-start | bytes 6148
  154.3 43.1 %all-to-all-start.4 = ((bf16[128,6,256]{2,1,0:T(8,128)(2,1)}), bf16[128,6,256]{2,1,0:T(8,128)(2,1)S(1)}, u32[]{:S(2)}, u32[]{:S(2)}) async-start(bf16[128,6,256]{2,1,0:T(8,128)(2,1)} %reshape.352), calls=%async_computation.4 | async-start | bytes 1048576 | tf_op jit(solution)/shard_map/all_to_all | solution.py:198
where the time goes:
time: 201 us; the launch traced here: 200 us
  starting transfers between devices  81.9 us (41%)
  waiting for transfers between devices  63.4 us (32%)
  local copies, waits for them, and re-layouts  34.5 us (17%)
  matrix products  11.3 us (6%)
  other arithmetic  7.81 us (4%)
    all_to_all x1, starting transfers between devices, per_device(): lax.all_to_all(sent_slot, 'seq', split_axis=0, concat_axis=0, tiled=True)  20.9 us
    all_to_all x1, waiting for transfers between devices, per_device(): lax.all_to_all(return_rows(results, arrival_flat), 'seq', split_axis=0, c...  20.8 us
    all_to_all x1, starting transfers between devices, per_device(): lax.all_to_all(return_rows(results, arrival_flat), 'seq', split_axis=0, c...  20.3 us
    all_to_all x1, starting transfers between devices, per_device(): lax.all_to_all(return_rows(out_blocks, arrival_flat), 'seq', split_axis=0...  16.8 us
    all_to_all x1, waiting for transfers between devices, per_device(): lax.all_to_all(pack_rows(out_grad), 'seq', split_axis=0, concat_axis=0, t...  12.3 us
    all_to_all x1, waiting for transfers between devices, per_device(): lax.all_to_all(sent_slot, 'seq', split_axis=0, concat_axis=0, tiled=True)  11.7 us
    ppermute x3, starting transfers between devices, from_behind(): return lax.ppermute(block, axis, route)  10.8 us
    all_to_all x1, waiting for transfers between devices, per_device(): lax.all_to_all(pack_rows(joined), 'seq', split_axis=0, concat_axis=0, til...  9.85 us
  transfers between devices with their start and end apart: 8, of which 7 were waited for; matrix products, arithmetic and copies ran while one was open for 12% of the time, Pallas kernels for 0%

commit v1 on v0

v1 whole, which is shorter than its diff:
```python
import jax
import jax.numpy as jnp
from jax import lax
from jax.experimental import pallas as pl
from jax.experimental.pallas import tpu as pltpu
from jax.sharding import PartitionSpec as P

HEAD_DIM = 64
BLOCK = 512
RANKS = 6
PEERS = 128
CHIPS = 64
ROWS = 24
TILE = 128

log2_e = 1.4426950408889634
self_score = -100000.0 * log2_e
masked_score = -1000000000.0 * log2_e
norm_eps = 1e-06

F32 = jnp.float32
BF16 = jnp.bfloat16
I32 = jnp.int32


def iota(shape, dim):
    return lax.broadcasted_iota(I32, shape, dim)


def mm(a, b):
    return jnp.dot(a, b, preferred_element_type=F32)


def ones_where(mask):
    return jnp.where(mask, F32(1), F32(0)).astype(BF16)


def column(row):
    return jnp.transpose(jnp.broadcast_to(row.astype(F32), (128, row.shape[1])))


def lanes_equal(index_col, width):
    lane = iota(index_col.shape, 1)
    return jnp.concatenate(
        [ones_where(index_col == lane + 128 * n) for n in range(width // 128)], axis=1
    )


def rows_equal(index_row, height):
    return ones_where(iota((height, index_row.shape[1]), 0) == index_row)


def pack_kernel(slot_ref, order_ref, q_ref, v_ref, g_ref, msg_ref, code_ref, order_out_ref):
    order_out_ref[...] = order_ref[...]
    block = slot_ref[...] >> 9
    local = block.shape[1]
    member = iota((PEERS, local), 0) == block
    before = ones_where(iota((local, local), 0) < iota((local, local), 1))
    counts = mm(ones_where(member), before)
    rank = jnp.sum(jnp.where(member, counts, F32(0)), axis=0, keepdims=True)
    code = block * 8 + rank.astype(I32)
    code_ref[...] = code

    def wanted(first, count):
        shape = (CHIPS, count, 128)
        base = 16 * iota(shape, 0)
        at = iota(shape, 1) + first
        prior = base - 8 + at
        prior = jnp.where(prior < 0, prior + 8 * PEERS, prior)
        qv = jnp.where(at < 6, prior, jnp.where(at < 12, base + at - 6, base + at - 4))
        ga = jnp.where(at >= 18, base + at - 18, -1)
        gb = jnp.where(at >= 18, base + at - 10, -1)
        qv = jnp.where(at < 18, qv, -1)
        return [x.reshape(CHIPS * count, 128) for x in (qv, ga, gb)]

    def choose(want):
        return jnp.concatenate(
            [ones_where(want == code[:, 128 * n : 128 * n + 128]) for n in range(local // 128)],
            axis=1,
        )

    q, v, g = q_ref[...], v_ref[...], g_ref[...]
    h0, h1 = slice(0, HEAD_DIM), slice(HEAD_DIM, 2 * HEAD_DIM)
    none = jnp.zeros((local, HEAD_DIM), BF16)
    qv = jnp.concatenate([q[:, h0], v[:, h0], q[:, h1], v[:, h1]], axis=1)
    ga = jnp.concatenate([g[:, h0], none, g[:, h1], none], axis=1)
    gb = jnp.concatenate([none, g[:, h0], none, g[:, h1]], axis=1)
    head = mm(choose(wanted(0, 16)[0]), qv)
    pick = jnp.concatenate([choose(w) for w in wanted(16, 8)], axis=1)
    tail = mm(pick, jnp.concatenate([qv, ga, gb], axis=0))
    for c in range(2):
        cols = slice(128 * c, 128 * c + 128)
        rows = jnp.concatenate(
            [head[:, cols].reshape(CHIPS, 16, 128), tail[:, cols].reshape(CHIPS, 8, 128)], axis=1
        )
        msg_ref[:, c] = rows.astype(BF16)


def meta_kernel(z_ref, a_ref, b_ref, code_ref, rows_ref, cols_ref):
    n = BLOCK
    lane = iota((n, n), 1)
    at = iota((1, n), 1)

    def wide(col):
        return jnp.concatenate([col] * (n // 128), axis=1)

    for i, ref in enumerate((z_ref, a_ref, b_ref)):
        pos = ref[...].astype(F32)
        pos_col = wide(column(pos))
        place = jnp.sum(jnp.where(pos_col < pos, F32(1), F32(0)), axis=0, keepdims=True)
        place_col = wide(column(place)).astype(I32)
        ordered = jnp.sum(jnp.where(place_col == lane, pos_col, F32(0)), axis=0, keepdims=True)
        ordered_col = column(ordered)
        source = ordered.astype(I32) >> 9
        start = (source << 9).astype(F32)
        offset = jnp.sum(
            jnp.where(wide(ordered_col) < start, F32(1), F32(0)), axis=0, keepdims=True
        )
        code = source * 8 + at - offset.astype(I32)
        rows_ref[i : i + 1] = ordered.astype(I32)
        rows_ref[i + 3 : i + 4] = code
        if i > 0:
            cols_ref[i - 1] = ordered_col.astype(I32)
        cols_ref[i + 2] = column(code).astype(I32)
    rows_ref[6:8] = jnp.zeros((2, n), I32)
    cols_ref[5] = column(code_ref[...]).astype(I32)


def attend_kernel(arr_ref, rows_ref, cols_ref, out_ref, p_ref, ds_ref):
    n = BLOCK
    arrived = arr_ref[...].astype(F32)
    part = [
        arrived[:, 8 * i : 8 * i + 8].reshape(8 * PEERS, 128).astype(BF16) for i in range(3)
    ]
    part01 = jnp.concatenate(part[:2], axis=0)
    part12 = jnp.concatenate(part[1:], axis=0)
    group = 8 * PEERS

    def place_a(code):
        return jnp.where((code & 7) < 2, code + 6, group + code - 2)

    def place_b(code):
        return jnp.where((code & 7) < 4, code + 4, group + code - 4)

    code_z, code_a, code_b = cols_ref[2], cols_ref[3], cols_ref[4]
    x_z = mm(lanes_equal(code_z, group), part[0])
    x_a = mm(lanes_equal(place_a(code_a), 2 * group), part01)
    x_b = mm(lanes_equal(place_b(code_b), 2 * group), part12)
    g_a = mm(lanes_equal(code_a + 2, group), part[2])[:, :HEAD_DIM]
    g_b = mm(lanes_equal(code_b + 2, group), part[2])[:, HEAD_DIM:]

    ones = jnp.ones((n, HEAD_DIM), F32)

    def block_of(x):
        turned = jnp.transpose(x)
        q_t, v_t = turned[:HEAD_DIM], turned[HEAD_DIM:]
        norm = lax.rsqrt(jnp.sum(q_t * q_t, axis=0, keepdims=True) + norm_eps)
        q = x[:, :HEAD_DIM]
        norm_col = lax.rsqrt(jnp.sum(q * q, axis=1, keepdims=True) + norm_eps)
        return dict(
            q=q.astype(BF16),
            q_t=q_t,
            q_tb=q_t.astype(BF16),
            v_tb=v_t.astype(BF16),
            norm=norm,
            scale=norm * log2_e,
            key=(q * norm_col).astype(BF16),
            ones_v=jnp.concatenate([ones, x[:, HEAD_DIM:]], axis=1).astype(BF16),
        )

    blocks = [block_of(x) for x in (x_z, x_a, x_b)]

    def item(prior, own, grads, prior_pos, own_pos):
        outs, query_grads, scaled_grads = [], [], []
        for t in range(n // TILE):
            lo, hi = t * TILE, (t + 1) * TILE
            q = own["q"][lo:hi]
            s_prior = mm(q, prior["q_tb"]) * prior["scale"]
            pos_col = jnp.concatenate([own_pos[lo:hi]] * (n // 128), axis=1)
            s_prior = jnp.where(prior_pos < pos_col, s_prior, masked_score)
            s_own = mm(q, own["q_tb"][:, :hi]) * own["scale"][:, :hi]
            row, col = iota((TILE, TILE), 0), iota((TILE, TILE), 1)
            last = jnp.where(
                col < row, s_own[:, lo:], jnp.where(col == row, self_score, masked_score)
            )
            s_own = jnp.concatenate([s_own[:, :lo], last], axis=1) if t else last
            top = jnp.maximum(
                jnp.max(s_prior, axis=1, keepdims=True), jnp.max(s_own, axis=1, keepdims=True)
            )
            p_prior = jnp.exp2(s_prior - top)
            p_own = jnp.exp2(s_own - top)
            pb_prior, pb_own = p_prior.astype(BF16), p_own.astype(BF16)
            summed = mm(pb_prior, prior["ones_v"]) + mm(pb_own, own["ones_v"][:hi])
            inverse = 1.0 / summed[:, :HEAD_DIM]
            out = (summed[:, HEAD_DIM:] * inverse).astype(BF16)
            grad = (grads[lo:hi] * inverse).astype(BF16)
            delta = jnp.sum(grad.astype(F32) * out.astype(F32), axis=1, keepdims=True)
            ds_prior = (p_prior * (mm(grad, prior["v_tb"]) - delta)).astype(BF16)
            ds_own = (p_own * (mm(grad, own["v_tb"][:, :hi]) - delta)).astype(BF16)
            query_grads.append(mm(ds_prior, prior["key"]) + mm(ds_own, own["key"][:hi]))
            outs.append(out)
            scaled_grads.append(grad)
            p_ref[lo:hi, :n] = pb_prior
            ds_ref[lo:hi, :n] = ds_prior
            p_ref[lo:hi, n : n + hi] = pb_own
            ds_ref[lo:hi, n : n + hi] = ds_own
            if hi < n:
                rest = jnp.zeros((TILE, n - hi), BF16)
                p_ref[lo:hi, n + hi :] = rest
                ds_ref[lo:hi, n + hi :] = rest
        grad_t = jnp.transpose(jnp.concatenate(scaled_grads, axis=0).astype(F32)).astype(BF16)
        half = n // 2

        def back(left, ref):
            whole = mm(left, ref[:, : n + half])
            late = mm(left[:, half:], ref[half:, n + half :])
            return whole[:, :n], jnp.concatenate([whole[:, n:], late], axis=1)

        dk_prior, dk_own = back(own["q_tb"], ds_ref)
        dv_prior, dv_own = back(grad_t, p_ref)
        return (
            jnp.concatenate(outs, axis=0),
            jnp.concatenate(query_grads, axis=0),
            (dk_prior, dv_prior),
            (dk_own, dv_own),
        )

    block_z, block_a, block_b = blocks
    pos_z, pos_a = rows_ref[0:1], rows_ref[1:2]
    out_a, dq_a, sums_z, sums_a = item(block_z, block_a, g_a, pos_z, cols_ref[0])
    out_b, dq_b, more_a, sums_b = item(block_a, block_b, g_b, pos_a, cols_ref[1])
    sums_a = (sums_a[0] + more_a[0], sums_a[1] + more_a[1])

    def result(block, sums, query_grad):
        dk, dv = sums
        norm, q_t = block["norm"], block["q_t"]
        along = jnp.sum(q_t * dk, axis=0, keepdims=True) * (norm * norm)
        dk = norm * (dk - along * q_t)
        both = jnp.transpose(jnp.concatenate([dk, dv], axis=0))
        if query_grad is not None:
            both = jnp.concatenate(
                [both[:, :HEAD_DIM] + query_grad, both[:, HEAD_DIM:]], axis=1
            )
        return both.astype(BF16)

    r_z = result(block_z, sums_z, None)
    r_a = result(block_a, sums_a, dq_a)
    r_b = result(block_b, sums_b, dq_b)
    none = jnp.zeros((n, HEAD_DIM), BF16)
    o_a = jnp.concatenate([out_a, none], axis=1)
    o_b = jnp.concatenate([none, out_b], axis=1)

    row_z, row_a, row_b = rows_ref[3:4], rows_ref[4:5], rows_ref[5:6]
    at_a, at_b = place_a(row_a), place_b(row_b)

    def send(places, values):
        chosen = jnp.concatenate([rows_equal(at, group) for at in places], axis=1)
        return mm(chosen, jnp.concatenate(values, axis=0)).reshape(PEERS, 8, 128)

    sent = [
        send([row_z, at_a], [r_z, r_a]),
        send([at_a - group, at_b], [r_a, r_b]),
        send([at_b - group, row_a + 2, row_b + 2], [r_b, o_a, o_b]),
    ]
    out_ref[...] = jnp.concatenate(sent, axis=1).astype(BF16)


def restore_kernel(ret_ref, code_ref, att_ref, dqk_ref, dv_ref):
    code = code_ref[0]
    block, rank = code >> 3, code & 7
    chip, odd = block >> 1, (block & 1) == 1
    group = 8 * CHIPS
    base = chip * 8 + rank
    even_at = jnp.where(rank < 2, base + 6, group + base - 2)
    odd_at = jnp.where(rank < 4, group + base + 4, 2 * group + base - 4)
    own_at = jnp.where(odd, odd_at, even_at)
    prior_at = jnp.where(odd, ((chip + 1) & (CHIPS - 1)) * 8 + rank, -1)
    lane = iota(code.shape, 1)
    chosen = jnp.concatenate(
        [
            ones_where((own_at == lane + 128 * i) | (prior_at == lane + 128 * i))
            for i in range(3 * group // 128)
        ],
        axis=1,
    )
    returned = ret_ref[...].astype(F32)
    values = [
        jnp.concatenate(
            [returned[:, c, 8 * i : 8 * i + 8].reshape(group, 128) for c in range(2)], axis=1
        ).astype(BF16)
        for i in range(3)
    ]
    grads = mm(chosen, jnp.concatenate(values, axis=0)).astype(BF16)
    outs = mm(lanes_equal(base + 2, group), values[2])
    h = HEAD_DIM
    odd_h = odd[:, :h]
    att_ref[...] = jnp.concatenate(
        [
            jnp.where(odd_h, outs[:, h : 2 * h], outs[:, :h]),
            jnp.where(odd_h, outs[:, 3 * h :], outs[:, 2 * h : 3 * h]),
        ],
        axis=1,
    ).astype(BF16)
    dqk_ref[...] = jnp.concatenate([grads[:, :h], grads[:, 2 * h : 3 * h]], axis=1)
    dv_ref[...] = jnp.concatenate([grads[:, h : 2 * h], grads[:, 3 * h :]], axis=1)


def struct(shape, dtype):
    return jax.ShapeDtypeStruct(shape, dtype)


def params(mib):
    return pltpu.CompilerParams(vmem_limit_bytes=mib * 1024 * 1024)


def pack(slots, order, q, v, g):
    n = q.shape[0]
    return pl.pallas_call(
        pack_kernel,
        out_shape=(
            struct((CHIPS, 2, ROWS, 128), BF16),
            struct((1, n), I32),
            struct((1, n), I32),
        ),
        compiler_params=params(32),
        name="pack",
    )(slots, order, q, v, g)


def meta(z, a, b, code):
    return pl.pallas_call(
        meta_kernel,
        out_shape=(struct((8, BLOCK), I32), struct((6, BLOCK, 128), I32)),
        compiler_params=params(32),
        name="meta",
    )(z, a, b, code)


def attend(arrived, rows, cols):
    return pl.pallas_call(
        attend_kernel,
        out_shape=struct((PEERS, ROWS, 128), BF16),
        scratch_shapes=[pltpu.VMEM((BLOCK, 2 * BLOCK), BF16)] * 2,
        compiler_params=params(48),
        name="attend",
    )(arrived, rows, cols)


def restore(returned, cols):
    n = cols.shape[1]
    return pl.pallas_call(
        restore_kernel,
        grid=(1,),
        in_specs=[
            pl.BlockSpec((CHIPS, 2, ROWS, 128), lambda i: (0, 0, 0, 0)),
            pl.BlockSpec((1, n, 128), lambda i: (5, 0, 0)),
        ],
        out_specs=[pl.BlockSpec((n, 128), lambda i: (0, 0))] * 3,
        out_shape=[struct((n, 128), BF16)] * 3,
        compiler_params=params(32),
        name="restore",
    )(returned, cols)


def exchange(message):
    return lax.all_to_all(message, "seq", split_axis=0, concat_axis=0, tiled=True)


def per_device(shared_qk, value_rows, out_grad, bucket_order, inverse_order):
    message, code, order = pack(inverse_order, bucket_order, shared_qk, value_rows, out_grad)
    arrived = exchange(message.reshape(PEERS, ROWS, 128))
    peers = range(PEERS)
    other = lax.ppermute(order, "seq", [(i, i ^ 1) for i in peers])
    first = lax.axis_index("seq") % 2 == 0
    order_a = jnp.where(first, order, other)
    order_b = jnp.where(first, other, order)
    order_z = lax.ppermute(order_b, "seq", [(i, (i + 2) % PEERS) for i in peers])
    rows, cols = meta(order_z, order_a, order_b, code)
    returned = exchange(attend(arrived, rows, cols))
    attended, grad_qk, grad_v = restore(returned.reshape(CHIPS, 2, ROWS, 128), cols)
    return attended, grad_qk, grad_v


def solution(mesh):
    rows, orders = P("seq", "head"), P("head", "seq")
    return jax.shard_map(
        per_device,
        mesh=mesh,
        in_specs=(rows, rows, rows, orders, orders),
        out_specs=(rows, rows, rows),
        check_vma=False,
    )
```

time: 201 us -> 102 us (0.51)
  starting transfers between devices: 81.9 us -> 26.6 us
  waiting for transfers between devices: 63.4 us -> 18 us
  blocking collectives: 0 us -> 35.1 us
  local copies, waits for them, and re-layouts: 34.5 us -> 4.07 us
  Pallas kernels: 0 us -> 16.7 us
  matrix products: 11.3 us -> 0 us
  other arithmetic: 7.81 us -> 0.01 us
    all_to_all x5 -> x1, waiting for transfers between devices: 54.6 us -> 1.33 us  [exchange(): lax.all_to_all(message, 'seq', split_axis=0, concat_axis=0, tiled=True)]
    all_to_all x5 -> x1, starting transfers between devices: 71.1 us -> 20.9 us  [exchange(): lax.all_to_all(message, 'seq', split_axis=0, concat_axis=0, tiled=True)]
    all_to_all x0 -> x1, blocking collectives: none -> 35.1 us  [exchange(): lax.all_to_all(message, 'seq', split_axis=0, concat_axis=0, tiled=True)]
    gather x10 -> x0, local copies, waits for them, and re-layouts: 20.2 us -> none  [the longest x2 5.17 us: return_rows(): padded[arrival_flat].reshape(peer_count, capacity, sorted_in.shape[1])]
    pallas_call x0 -> x4, Pallas kernels: none -> 16.7 us  [the longest x1 11.1 us: attend(): pl.pallas_call(attend_kernel, out_shape=struct((PEERS, ROWS, 128), BF16),...]
    dot_general x12 -> x0, matrix products: 11.3 us -> none  [the longest x2 3.76 us: head_grads(): jnp.dot(grad_rows, value_keys.T, preferred_element_type=jnp.float32)]
    ppermute x3 -> x2, waiting for transfers between devices: 8.81 us -> 16.6 us  [the longest x1 15.8 us: per_device(): lax.ppermute(order_b, 'seq', [(i, (i + 2) % PEERS) for i in peers])]
    scatter x2 -> x0, local copies, waits for them, and re-layouts: 6 us -> none  [the longest x1 3.56 us: unpack_rows(): where_from = jnp.full((local_rows + 1,), peer_count * capacity, jnp.int32...]
  transfers between devices with their start and end apart: 8 -> 3, of which waited for: 7 -> 3; matrix products, arithmetic and copies ran while one was open for 12% -> 0% of each run, Pallas kernels for 0% -> 2%
where the time goes in v1:
time: 102 us; the launch traced here: 101 us
  blocking collectives  35.1 us (34%)
  starting transfers between devices  26.6 us (26%)
  waiting for transfers between devices  18 us (18%)
  Pallas kernels  16.7 us (16%)
  local copies, waits for them, and re-layouts  4.07 us (4%)
    all_to_all x1, blocking collectives, exchange(): lax.all_to_all(message, 'seq', split_axis=0, concat_axis=0, tiled=True)  35.1 us
    all_to_all x1, starting transfers between devices, exchange(): lax.all_to_all(message, 'seq', split_axis=0, concat_axis=0, tiled=True)  20.9 us
    ppermute x1, waiting for transfers between devices, per_device(): lax.ppermute(order_b, 'seq', [(i, (i + 2) % PEERS) for i in peers])  15.8 us
    pallas_call x1, Pallas kernels, attend(): pl.pallas_call(attend_kernel, out_shape=struct((PEERS, ROWS, 128), BF16),...  11.1 us
    unnamed x10, local copies, waits for them, and re-layouts  4.07 us
    ppermute x1, starting transfers between devices, per_device(): lax.ppermute(order_b, 'seq', [(i, (i + 2) % PEERS) for i in peers])  2.93 us
    ppermute x1, starting transfers between devices, per_device(): other = lax.ppermute(order, 'seq', [(i, i ^ 1) for i in peers])  2.8 us
  transfers between devices with their start and end apart: 3, of which 3 were waited for; matrix products, arithmetic and copies ran while one was open for 0% of the time, Pallas kernels for 2%

profile of v1, /device:TPU:1, one launch (start us, length us, event | category | flops | bytes accessed | tf_op | source)
XLA Modules:
  0.0 101.1 jit_solution(6768678748001946757)
XLA Ops:
  0.6 0.0 copy-start
  0.6 0.9 copy-done
  1.5 0.0 copy-start.1
  1.5 0.9 copy-done.1
  2.4 0.0 copy-start.2
  2.4 0.9 copy-done.2
  3.3 0.0 copy-start.3
  3.3 0.7 copy-done.3
  4.0 0.0 copy-start.4
  4.0 0.7 copy-done.4
  4.7 2.0 %pack.1 = (bf16[64,2,24,128]{3,2,1,0:T(8,128)(2,1)}, s32[1,512]{1,0:T(1,128)S(1)}, s32[1,512]{1,0:T(1,128)S(1)}) custom-call(s32[1,512]{1,0:T(1,128)S(1)} %copy-done.3, s32[1,512]{1,0:T(1,128)S(1)} %copy-done.4, bf16[512,128]{1,0:T(8,128)(2,1)S(1)} %copy-done, bf16[512,128]{1,0:T(8,128)(2,1)S(1)} %copy-done.1, bf16[512,128]{1,0:T(8,128)(2,1)S(1)} %copy-done.2), custom_call_target="tpu_custom_call" | custom-call | tf_op jit(solution)/shard_map/pack/pallas_call | solution.py:318
  6.7 20.9 %all-to-all-start = ((bf16[128,24,128]{2,1,0:T(8,128)(2,1)}), bf16[128,24,128]{2,1,0:T(8,128)(2,1)S(1)}, u32[]{:S(2)}, u32[]{:S(2)}) async-start(bf16[128,24,128]{2,1,0:T(8,128)(2,1)} %bitcast), calls=%async_computation | async-start | bytes 1572864 | tf_op jit(solution)/shard_map/all_to_all | solution.py:366
  27.6 2.8 %collective-permute-start = (s32[1,512]{1,0:T(1,128)S(1)}, s32[1,512]{1,0:T(1,128)S(1)}, u32[]{:S(2)}, u32[]{:S(2)}) collective-permute-start(s32[1,512]{1,0:T(1,128)S(1)} %get-tuple-element.9), channel_id=1, source_target_pairs={{0,4},{4,0},{8,12},{12,8},{16,20},{20,16},{24,28},{28,24},{32,36},... | collective-permute-start | bytes 6152 | tf_op jit(solution)/shard_map/ppermute | solution.py:373
  30.4 0.8 collective-permute-done
  31.2 2.9 %collective-permute-start.1 = (s32[1,512]{1,0:T(1,128)S(1)}, s32[1,512]{1,0:T(1,128)S(1)}, u32[]{:S(2)}, u32[]{:S(2)}) collective-permute-start(s32[1,512]{1,0:T(1,128)S(1)} %get-tuple-element.14.b_ref), channel_id=1, source_target_pairs={{0,8},{4,12},{8,16},{12,20},{16,24},{20,28},{24,32},{28,36},{32,40... | collective-permute-start | bytes 6152 | tf_op jit(solution)/shard_map/ppermute | solution.py:377
  34.1 15.8 %collective-permute-done.1.z_ref = s32[1,512]{1,0:T(1,128)S(1)} collective-permute-done((s32[1,512]{1,0:T(1,128)S(1)}, s32[1,512]{1,0:T(1,128)S(1)}, u32[]{:S(2)}, u32[]{:S(2)}) %collective-permute-start.1) | collective-permute-done | bytes 2080 | tf_op jit(solution)/shard_map/ppermute | solution.py:377
  50.0 1.8 %meta.1 = (s32[8,512]{1,0:T(8,128)S(1)}, s32[6,512,128]{2,1,0:T(8,128)S(1)}) custom-call(s32[1,512]{1,0:T(1,128)S(1)} %collective-permute-done.1.z_ref, s32[1,512]{1,0:T(1,128)S(1)} %get-tuple-element.13.a_ref, s32[1,512]{1,0:T(1,128)S(1)} %get-tuple-element.14.b_ref, s32[1,512]{1,0:T(1,128)S(1)} %get-tuple-element.10.code_ref), custom_call_target="tpu_custom_call" | custom-call | tf_op jit(solution)/shard_map/meta/pallas_call | solution.py:331
  51.8 1.3 %all-to-all-done.arr_ref = bf16[128,24,128]{2,1,0:T(8,128)(2,1)S(1)} async-done(((bf16[128,24,128]{2,1,0:T(8,128)(2,1)}), bf16[128,24,128]{2,1,0:T(8,128)(2,1)S(1)}, u32[]{:S(2)}, u32[]{:S(2)}) %all-to-all-start) | async-done | bytes 786464 | tf_op jit(solution)/shard_map/all_to_all | solution.py:366
  53.1 11.1 %attend.1 = bf16[128,24,128]{2,1,0:T(8,128)(2,1)S(1)} custom-call(bf16[128,24,128]{2,1,0:T(8,128)(2,1)S(1)} %all-to-all-done.arr_ref, s32[8,512]{1,0:T(8,128)S(1)} %get-tuple-element.11.rows_ref, s32[6,512,128]{2,1,0:T(8,128)S(1)} %get-tuple-element.12.cols_ref.code_ref), custom_call_target="tpu_custom_call" | custom-call | tf_op jit(solution)/shard_map/attend/pallas_call | solution.py:340
  64.2 35.1 %all_to_all.10 = bf16[128,24,128]{2,1,0:T(8,128)(2,1)S(1)} all-to-all(bf16[128,24,128]{2,1,0:T(8,128)(2,1)S(1)} %attend.1), channel_id=1, replica_groups=mesh['seq'=128,'head'=4] {'seq'}, dimensions={0} | all-to-all | bytes 1572864 | tf_op jit(solution)/shard_map/all_to_all | solution.py:366
  99.3 1.8 %restore.1 = (bf16[512,128]{1,0:T(8,128)(2,1)}, bf16[512,128]{1,0:T(8,128)(2,1)}, bf16[512,128]{1,0:T(8,128)(2,1)}) custom-call(bf16[64,2,24,128]{3,2,1,0:T(8,128)(2,1)S(1)} %bitcast.2, s32[6,512,128]{2,1,0:T(8,128)S(1)} %get-tuple-element.12.cols_ref.code_ref), custom_call_target="tpu_custom_call" | custom-call | tf_op jit(solution)/shard_map/restore/pallas_call | solution.py:351
  (1 shorter events, 0.0 us)
Async XLA Ops:
  0.6 0.9 copy-start
  1.5 0.9 copy-start.1
  2.4 0.9 copy-start.2
  3.3 0.7 copy-start.3
  4.0 0.7 copy-start.4
  6.7 46.4 %all-to-all-start = ((bf16[128,24,128]{2,1,0:T(8,128)(2,1)}), bf16[128,24,128]{2,1,0:T(8,128)(2,1)S(1)}, u32[]{:S(2)}, u32[]{:S(2)}) async-start(bf16[128,24,128]{2,1,0:T(8,128)(2,1)} %bitcast), calls=%async_computation | async-start | bytes 1572864 | tf_op jit(solution)/shard_map/all_to_all | solution.py:366
  27.6 3.6 %collective-permute-start = (s32[1,512]{1,0:T(1,128)S(1)}, s32[1,512]{1,0:T(1,128)S(1)}, u32[]{:S(2)}, u32[]{:S(2)}) collective-permute-start(s32[1,512]{1,0:T(1,128)S(1)} %get-tuple-element.9), channel_id=1, source_target_pairs={{0,4},{4,0},{8,12},{12,8},{16,20},{20,16},{24,28},{28,24},{32,36},... | collective-permute-start | bytes 6152 | tf_op jit(solution)/shard_map/ppermute | solution.py:373
  31.2 18.8 %collective-permute-start.1 = (s32[1,512]{1,0:T(1,128)S(1)}, s32[1,512]{1,0:T(1,128)S(1)}, u32[]{:S(2)}, u32[]{:S(2)}) collective-permute-start(s32[1,512]{1,0:T(1,128)S(1)} %get-tuple-element.14.b_ref), channel_id=1, source_target_pairs={{0,8},{4,12},{8,16},{12,20},{16,24},{20,28},{24,32},{28,36},{32,40... | collective-permute-start | bytes 6152 | tf_op jit(solution)/shard_map/ppermute | solution.py:377

commit v2 on v1

v2 whole, which is shorter than its diff:
```python
import jax
import jax.numpy as jnp
from jax import lax
from jax.experimental import pallas as pl
from jax.experimental.pallas import tpu as pltpu
from jax.sharding import PartitionSpec as P

HEAD_DIM = 64
BLOCK = 512
RANKS = 6
PEERS = 128
CHIPS = 64
ROWS = 24

META_FLOPS = 12 * 10**9

log2_e = 1.4426950408889634
self_score = -100000.0 * log2_e
masked_score = -1000000000.0 * log2_e
norm_eps = 1e-06

F32 = jnp.float32
BF16 = jnp.bfloat16
I32 = jnp.int32


def iota(shape, dim):
    return lax.broadcasted_iota(I32, shape, dim)


def mm(a, b):
    return jnp.dot(a, b, preferred_element_type=F32)


def ones_where(mask):
    return jnp.where(mask, F32(1), F32(0)).astype(BF16)


def column(row):
    return jnp.transpose(jnp.broadcast_to(row.astype(F32), (128, row.shape[1])))


def lanes_equal(index_col, width):
    lane = iota(index_col.shape, 1)
    return jnp.concatenate(
        [ones_where(index_col == lane + 128 * n) for n in range(width // 128)], axis=1
    )


def rows_equal(index_row, height):
    return ones_where(iota((height, index_row.shape[1]), 0) == index_row)


def tiles_of(rows):
    count = rows.shape[0] * 8
    mixed = jnp.concatenate(
        [rows[:, 6:8], rows[:, 14:16], rows[:, 22:24], jnp.zeros_like(rows[:, :2])], axis=1
    )
    tiles = [rows[:, 8 * i : 8 * i + 8] for i in range(3)] + [mixed]
    return [t.reshape(count, 128).astype(BF16) for t in tiles]


def rows_of(tiles, mixed):
    pieces = []
    for i, tile in enumerate(tiles):
        pieces += [tile[:, :6], mixed[:, 2 * i : 2 * i + 2]]
    return jnp.concatenate(pieces, axis=1).astype(BF16)


def pack_kernel(slot_hbm, q_hbm, v_hbm, g_hbm, msg_ref, code_ref, slot_ref, q_ref, v_ref, g_ref, sems):
    copies = [
        pltpu.make_async_copy(src, dst, sems.at[i])
        for i, (src, dst) in enumerate(
            [(slot_hbm, slot_ref), (q_hbm, q_ref), (v_hbm, v_ref), (g_hbm, g_ref)]
        )
    ]
    for copy in copies:
        copy.start()
    copies[0].wait()
    block = slot_ref[...] >> 9
    local = block.shape[1]
    member = iota((PEERS, local), 0) == block
    before = ones_where(iota((local, local), 0) < iota((local, local), 1))
    counts = mm(ones_where(member), before)
    rank = jnp.sum(jnp.where(member, counts, F32(0)), axis=0, keepdims=True)
    code = block * 8 + rank.astype(I32)
    code_ref[...] = code

    def choose(offset):
        shape = (CHIPS, 8, 128)
        want = 16 * iota(shape, 0) + iota(shape, 1) + offset
        want = jnp.where(want < 0, want + 8 * PEERS, want).reshape(CHIPS * 8, 128)
        return jnp.concatenate(
            [ones_where(want == code[:, 128 * n : 128 * n + 128]) for n in range(local // 128)],
            axis=1,
        )

    chosen = [choose(offset) for offset in (-8, 0, 8)]
    for copy in copies[1:]:
        copy.wait()
    q, v, g = q_ref[...], v_ref[...], g_ref[...]
    h0, h1 = slice(0, HEAD_DIM), slice(HEAD_DIM, 2 * HEAD_DIM)
    none = jnp.zeros((local, HEAD_DIM), BF16)
    qv = jnp.concatenate([q[:, h0], v[:, h0], q[:, h1], v[:, h1]], axis=1)
    ga = jnp.concatenate([g[:, h0], none, g[:, h1], none], axis=1)
    gb = jnp.concatenate([none, g[:, h0], none, g[:, h1]], axis=1)
    tiles = [mm(one, qv) for one in chosen]
    mixed = mm(jnp.concatenate(chosen[1:], axis=1), jnp.concatenate([ga, gb], axis=0))
    for c in range(2):
        cols = slice(128 * c, 128 * c + 128)
        msg_ref[:, c] = rows_of(
            [t[:, cols].reshape(CHIPS, 8, 128) for t in tiles],
            mixed[:, cols].reshape(CHIPS, 8, 128),
        )


def meta_kernel(orders_ref, code_ref, table_ref):
    n = BLOCK
    lane = iota((n, n), 1)
    at = iota((1, n), 1)

    def wide(col):
        return jnp.concatenate([col] * (n // 128), axis=1)

    for i in range(3):
        pos = orders_ref[i : i + 1].astype(F32)
        pos_col = wide(column(pos))
        place = jnp.sum(jnp.where(pos_col < pos, F32(1), F32(0)), axis=0, keepdims=True)
        place_col = wide(column(place)).astype(I32)
        ordered = jnp.sum(jnp.where(place_col == lane, pos_col, F32(0)), axis=0, keepdims=True)
        source = ordered.astype(I32) >> 9
        start = (source << 9).astype(F32)
        offset = jnp.sum(
            jnp.where(wide(column(ordered)) < start, F32(1), F32(0)), axis=0, keepdims=True
        )
        table_ref[i : i + 1] = ordered.astype(I32)
        table_ref[i + 3 : i + 4] = source * 8 + at - offset.astype(I32)
    table_ref[6:7] = code_ref[...]
    table_ref[7:8] = jnp.zeros((1, n), I32)


def nt(a, b):
    return lax.dot_general(a, b, (((1,), (1,)), ((), ())), preferred_element_type=F32)


def tn(a, b):
    return lax.dot_general(a, b, (((0,), (0,)), ((), ())), preferred_element_type=F32)


def two_terms(x):
    high = x.astype(BF16)
    return high, (x - high.astype(F32)).astype(BF16)


def attend_kernel(arr_ref, table_hbm, out_ref, give_ref, rows_ref, sem):
    n, half, group = BLOCK, BLOCK // 2, 8 * PEERS
    fetch = pltpu.make_async_copy(table_hbm, rows_ref, sem)
    fetch.start()
    part_z, part_a, part_b, part_g = tiles_of(arr_ref[...].astype(F32))
    fetch.wait()
    reach = 3 * group // 4

    def take(i, part):
        code = rows_ref[3 + i : 4 + i]
        first, last = slice(0, half), slice(half, n)
        give_ref[i, :reach, first] = rows_equal(code[:, first], reach)
        give_ref[i, group - reach :, last] = rows_equal(code[:, last] - (group - reach), reach)
        return jnp.concatenate(
            [
                tn(part[:reach], give_ref[i, :reach, first]),
                tn(part[group - reach :], give_ref[i, group - reach :, last]),
            ],
            axis=1,
        )

    x_z = take(0, part_z)
    x_a = take(1, jnp.concatenate([part_a, part_g], axis=1))
    x_b = take(2, jnp.concatenate([part_b, part_g], axis=1))
    h = HEAD_DIM
    g_a, g_b = x_a[2 * h : 3 * h], x_b[3 * h :]
    pad = jnp.zeros((14, n), BF16)
    ones = jnp.ones((16, n), BF16)

    def block_of(x):
        q, v = x[:h], x[h : 2 * h]
        norm = lax.rsqrt(jnp.sum(q * q, axis=0, keepdims=True) + norm_eps)
        return dict(
            q=q,
            qb=q.astype(BF16),
            vb=jnp.concatenate([v.astype(BF16), ones], axis=0),
            norm=norm,
            scale=norm * log2_e,
            key=(q * norm).astype(BF16),
        )

    block_z, block_a, block_b = [block_of(x) for x in (x_z, x_a, x_b)]

    def item(prior, own, grads, prior_pos, own_pos):
        pos = jnp.concatenate([column(own_pos)] * (n // 128), axis=1)
        s_prior = tn(own["qb"], prior["qb"]) * prior["scale"]
        s_prior = jnp.where(prior_pos.astype(F32) < pos, s_prior, masked_score)
        s_own = tn(own["qb"], own["qb"]) * own["scale"]
        row, col = iota((n, n), 0), iota((n, n), 1)
        s_own = jnp.where(col < row, s_own, jnp.where(col == row, self_score, masked_score))
        top = jnp.maximum(
            jnp.max(s_prior, axis=1, keepdims=True), jnp.max(s_own, axis=1, keepdims=True)
        )
        p_prior = jnp.exp2(s_prior - top)
        p_own = jnp.exp2(s_own - top)
        pb_prior, pb_own = p_prior.astype(BF16), p_own.astype(BF16)
        summed = nt(prior["vb"], pb_prior) + nt(own["vb"], pb_own)
        inverse = 1.0 / summed[h : h + 1]
        out = (summed[:h] * inverse).astype(BF16)
        grad = (grads * inverse).astype(BF16)
        delta = jnp.sum(grad.astype(F32) * out.astype(F32), axis=0, keepdims=True)
        left = jnp.concatenate([grad, *two_terms(-delta), pad], axis=0)
        ds_prior = (p_prior * tn(left, prior["vb"])).astype(BF16)
        ds_own = (p_own * tn(left, own["vb"])).astype(BF16)
        dq = nt(prior["key"], ds_prior) + nt(own["key"], ds_own)
        sums_prior = (mm(own["qb"], ds_prior), mm(grad, pb_prior))
        sums_own = (mm(own["qb"], ds_own), mm(grad, pb_own))
        return out, dq, sums_prior, sums_own

    pos_z, pos_a, pos_b = rows_ref[0:1], rows_ref[1:2], rows_ref[2:3]
    out_a, dq_a, sums_z, sums_a = item(block_z, block_a, g_a, pos_z, pos_a)
    out_b, dq_b, more_a, sums_b = item(block_a, block_b, g_b, pos_a, pos_b)
    sums_a = (sums_a[0] + more_a[0], sums_a[1] + more_a[1])

    def result(block, sums, query_grad):
        dk, dv = sums
        norm, q = block["norm"], block["q"]
        along = jnp.sum(q * dk, axis=0, keepdims=True) * (norm * norm)
        dk = norm * (dk - along * q)
        if query_grad is not None:
            dk = dk + query_grad
        return [dk.astype(BF16), dv.astype(BF16)]

    def send(i, pieces):
        turned = jnp.concatenate(pieces, axis=0)
        sent = []
        for t, (lo, hi) in enumerate([(0, half), (0, n), (0, n), (half, n)]):
            sent.append(nt(give_ref[i, t * group // 4 : (t + 1) * group // 4, lo:hi], turned[:, lo:hi]))
        return jnp.concatenate(sent, axis=0)

    give_ref[:, reach:, :half] = jnp.zeros((3, group - reach, half), BF16)
    give_ref[:, : group - reach, half:] = jnp.zeros((3, group - reach, half), BF16)
    none = jnp.zeros((h, n), BF16)
    s_z = send(0, result(block_z, sums_z, None)).reshape(PEERS, 8, 128)
    s_a = send(1, [*result(block_a, sums_a, dq_a), out_a, none])
    s_b = send(2, [*result(block_b, sums_b, dq_b), none, out_b])
    mixed = (s_a[:, 128:] + s_b[:, 128:]).reshape(PEERS, 8, 128)
    s_a, s_b = (s[:, :128].reshape(PEERS, 8, 128) for s in (s_a, s_b))
    out_ref[...] = rows_of([s_z, s_a, s_b], mixed)


def restore_kernel(ret_ref, code_ref, att_ref, dqk_ref, dv_ref):
    code = column(code_ref[...]).astype(I32)
    block, rank = code >> 3, code & 7
    chip, odd = block >> 1, (block & 1) == 1
    group = 8 * CHIPS
    own_at = chip * 8 + rank
    prior_at = jnp.where(odd, ((chip + 1) & (CHIPS - 1)) * 8 + rank, -1)
    chosen = jnp.concatenate(
        [
            lanes_equal(prior_at, group),
            lanes_equal(jnp.where(odd, -1, own_at), group),
            lanes_equal(jnp.where(odd, own_at, -1), group),
        ],
        axis=1,
    )
    tiles = [tiles_of(ret_ref[:, c].astype(F32)) for c in range(2)]
    values = [jnp.concatenate([t[i] for t in tiles], axis=1) for i in range(4)]
    grads = mm(chosen, jnp.concatenate(values[:3], axis=0)).astype(BF16)
    outs = mm(lanes_equal(own_at, group), values[3])
    h = HEAD_DIM
    odd_h = odd[:, :h]
    att_ref[...] = jnp.concatenate(
        [
            jnp.where(odd_h, outs[:, h : 2 * h], outs[:, :h]),
            jnp.where(odd_h, outs[:, 3 * h :], outs[:, 2 * h : 3 * h]),
        ],
        axis=1,
    ).astype(BF16)
    dqk_ref[...] = jnp.concatenate([grads[:, :h], grads[:, 2 * h : 3 * h]], axis=1)
    dv_ref[...] = jnp.concatenate([grads[:, h : 2 * h], grads[:, 3 * h :]], axis=1)


def struct(shape, dtype):
    return jax.ShapeDtypeStruct(shape, dtype)


def params(mib):
    return pltpu.CompilerParams(vmem_limit_bytes=mib * 1024 * 1024)


def in_hbm(x):
    return pltpu.with_memory_space_constraint(x, pltpu.HBM)


def pack(slots, q, v, g):
    n = q.shape[0]
    return pl.pallas_call(
        pack_kernel,
        in_specs=[pl.BlockSpec(memory_space=pltpu.HBM)] * 4,
        out_shape=(struct((CHIPS, 2, ROWS, 128), BF16), struct((1, n), I32)),
        scratch_shapes=[pltpu.VMEM((1, n), I32)]
        + [pltpu.VMEM((n, 128), BF16)] * 3
        + [pltpu.SemaphoreType.DMA((4,))],
        compiler_params=params(24),
        name="pack",
    )(*map(in_hbm, (slots, q, v, g)))


def meta(orders, code):
    return pl.pallas_call(
        meta_kernel,
        out_shape=struct((8, BLOCK), I32),
        compiler_params=params(24),
        cost_estimate=pl.CostEstimate(
            flops=META_FLOPS, bytes_accessed=32768, transcendentals=0
        ),
        name="meta",
    )(orders, code)


def attend(arrived, table):
    return pl.pallas_call(
        attend_kernel,
        in_specs=[pl.BlockSpec(memory_space=pltpu.VMEM), pl.BlockSpec(memory_space=pltpu.HBM)],
        out_shape=struct((PEERS, ROWS, 128), BF16),
        scratch_shapes=[
            pltpu.VMEM((3, 8 * PEERS, BLOCK), BF16),
            pltpu.VMEM((8, BLOCK), I32),
            pltpu.SemaphoreType.DMA(()),
        ],
        compiler_params=params(40),
        name="attend",
    )(arrived, in_hbm(table))


def restore(returned, code):
    n = code.shape[1]
    return pl.pallas_call(
        restore_kernel,
        out_shape=[struct((n, 128), BF16)] * 3,
        compiler_params=params(24),
        name="restore",
    )(returned, code)


def exchange(message):
    return lax.all_to_all(message, "seq", split_axis=0, concat_axis=0, tiled=True)


def per_device(shared_qk, value_rows, out_grad, bucket_order, inverse_order):
    peers = range(PEERS)
    before = lax.ppermute(bucket_order, "seq", [(i, (i + 2) % PEERS) for i in peers])
    held = jnp.concatenate([bucket_order, before], axis=0)
    other = lax.ppermute(held, "seq", [(i, i ^ 1) for i in peers])
    even = lax.axis_index("seq") & 1 == 0
    near = jnp.concatenate(
        [
            jnp.where(even, other[1:], before),
            jnp.where(even, bucket_order, other[:1]),
            jnp.where(even, other[:1], bucket_order),
        ],
        axis=0,
    )
    message, code = pack(inverse_order, shared_qk, value_rows, out_grad)
    arrived = exchange(message.reshape(PEERS, ROWS, 128))
    returned = exchange(attend(arrived, meta(near, code)))
    return tuple(restore(returned.reshape(CHIPS, 2, ROWS, 128), code))


def solution(mesh):
    rows, orders = P("seq", "head"), P("head", "seq")
    return jax.shard_map(
        per_device,
        mesh=mesh,
        in_specs=(rows, rows, rows, orders, orders),
        out_specs=(rows, rows, rows),
        check_vma=False,
    )
```

time: 102 us -> 98.2 us (0.963)
  Pallas kernels: 16.7 us -> 12.7 us
  local copies, waits for them, and re-layouts: 4.07 us -> 0.61 us
  waiting for transfers between devices: 18 us -> 20.8 us
    all_to_all x1, waiting for transfers between devices: 1.33 us -> 20 us  [exchange(): lax.all_to_all(message, 'seq', split_axis=0, concat_axis=0, tiled=True)]
    ppermute x2, waiting for transfers between devices: 16.6 us -> 0.8 us  [the longest x1 0.79 us: per_device(): other = lax.ppermute(held, 'seq', [(i, i ^ 1) for i in peers])]
    pallas_call x4, Pallas kernels: 16.7 us -> 12.7 us  [the longest x1 6.79 us: attend(): pl.pallas_call(attend_kernel, in_specs=[pl.BlockSpec(memory_space=pltpu.V...]
    unnamed x10 -> x4, local copies, waits for them, and re-layouts: 4.07 us -> 0.61 us
    ppermute x2, starting transfers between devices: 5.73 us -> 7.63 us  [the longest x1 4.83 us: per_device(): lax.ppermute(bucket_order, 'seq', [(i, (i + 2) % PEERS) for i in peers])]
    all_to_all x1, starting transfers between devices: 20.9 us -> 19.4 us  [exchange(): lax.all_to_all(message, 'seq', split_axis=0, concat_axis=0, tiled=True)]
  transfers between devices with their start and end apart: 3 -> 3, of which waited for: 3 -> 2; matrix products, arithmetic and copies ran while one was open for 0% -> 0% of each run, Pallas kernels for 2% -> 4%
where the time goes in v2:
time: 98.2 us; the launch traced here: 97.8 us
  blocking collectives  35.9 us (37%)
  starting transfers between devices  27.1 us (28%)
  waiting for transfers between devices  20.8 us (21%)
  Pallas kernels  12.7 us (13%)
    all_to_all x1, blocking collectives, exchange(): lax.all_to_all(message, 'seq', split_axis=0, concat_axis=0, tiled=True)  35.9 us
    all_to_all x1, waiting for transfers between devices, exchange(): lax.all_to_all(message, 'seq', split_axis=0, concat_axis=0, tiled=True)  20 us
    all_to_all x1, starting transfers between devices, exchange(): lax.all_to_all(message, 'seq', split_axis=0, concat_axis=0, tiled=True)  19.4 us
    pallas_call x1, Pallas kernels, attend(): pl.pallas_call(attend_kernel, in_specs=[pl.BlockSpec(memory_space=pltpu.V...  6.79 us
    ppermute x1, starting transfers between devices, per_device(): lax.ppermute(bucket_order, 'seq', [(i, (i + 2) % PEERS) for i in peers])  4.83 us
    pallas_call x1, Pallas kernels, pack(): pl.pallas_call(pack_kernel, in_specs=[pl.BlockSpec(memory_space=pltpu.HBM...  2.97 us
    ppermute x1, starting transfers between devices, per_device(): other = lax.ppermute(held, 'seq', [(i, i ^ 1) for i in peers])  2.8 us
  transfers between devices with their start and end apart: 3, of which 2 were waited for; matrix products, arithmetic and copies ran while one was open for 0% of the time, Pallas kernels for 4%

profile of v2, /device:TPU:1, one launch (start us, length us, event | category | flops | bytes accessed | tf_op | source)
XLA Modules:
  0.0 97.8 jit_solution(3088964364994442384)
XLA Ops:
  0.6 4.8 %collective-permute-start = (s32[1,512]{1,0:T(1,128)}, s32[1,512]{1,0:T(1,128)S(1)}, u32[]{:S(2)}, u32[]{:S(2)}) collective-permute-start(s32[1,512]{1,0:T(1,128)} %param.8), channel_id=1, source_target_pairs={{0,8},{4,12},{8,16},{12,20},{16,24},{20,28},{24,32},{28,36},{32,40... | collective-permute-start | bytes 6152 | tf_op jit(solution)/shard_map/ppermute | solution.py:357
  5.5 3.0 %pack.1 = (bf16[64,2,24,128]{3,2,1,0:T(8,128)(2,1)}, s32[1,512]{1,0:T(1,128)S(1)}) custom-call(s32[1,512]{1,0:T(1,128)} %slot_hbm.1, bf16[512,128]{1,0:T(8,128)(2,1)} %q_hbm.1, bf16[512,128]{1,0:T(8,128)(2,1)} %v_hbm.1, bf16[512,128]{1,0:T(8,128)(2,1)} %g_hbm.1), custom_call_target="tpu_custom_call" | custom-call | tf_op jit(solution)/shard_map/pack/pallas_call | solution.py:302
  8.4 0.0 copy-start.1
  8.5 19.4 %all-to-all-start = ((bf16[128,24,128]{2,1,0:T(8,128)(2,1)}), bf16[128,24,128]{2,1,0:T(8,128)(2,1)S(1)}, u32[]{:S(2)}, u32[]{:S(2)}) async-start(bf16[128,24,128]{2,1,0:T(8,128)(2,1)} %bitcast), calls=%async_computation | async-start | bytes 1572864 | tf_op jit(solution)/shard_map/all_to_all | solution.py:352
  27.9 0.0 collective-permute-done
  27.9 0.0 copy-done.1
  27.9 2.8 %collective-permute-start.1 = (s32[2,512]{1,0:T(2,128)S(1)}, s32[2,512]{1,0:T(2,128)S(1)}, u32[]{:S(2)}, u32[]{:S(2)}) collective-permute-start(s32[2,512]{1,0:T(2,128)S(1)} %pad_add_fusion.1), channel_id=1, source_target_pairs={{0,4},{4,0},{8,12},{12,8},{16,20},{20,16},{24,28},{28,24},{32,36},... | collective-permute-start | bytes 12296 | tf_op jit(solution)/shard_map/ppermute | solution.py:359
  30.8 0.8 collective-permute-done.1
  31.6 1.3 %meta.1.table_hbm = s32[8,512]{1,0:T(8,128)S(1)} custom-call(s32[3,512]{1,0:T(4,128)S(1)} %pad_add_fusion.orders_ref, s32[1,512]{1,0:T(1,128)S(1)} %get-tuple-element.6.code_ref), custom_call_target="tpu_custom_call" | custom-call | flops 12000000000 | bytes 32768 | tf_op jit(solution)/shard_map/meta/pallas_call | solution.py:315
  32.8 0.0 copy-start
  32.8 0.6 copy-done
  33.4 20.0 %all-to-all-done.arr_ref = bf16[128,24,128]{2,1,0:T(8,128)(2,1)S(1)} async-done(((bf16[128,24,128]{2,1,0:T(8,128)(2,1)}), bf16[128,24,128]{2,1,0:T(8,128)(2,1)S(1)}, u32[]{:S(2)}, u32[]{:S(2)}) %all-to-all-start) | async-done | bytes 786464 | tf_op jit(solution)/shard_map/all_to_all | solution.py:352
  53.4 6.8 %attend.1 = bf16[128,24,128]{2,1,0:T(8,128)(2,1)S(1)} custom-call(bf16[128,24,128]{2,1,0:T(8,128)(2,1)S(1)} %all-to-all-done.arr_ref, s32[8,512]{1,0:T(8,128)} %copy-done), custom_call_target="tpu_custom_call" | custom-call | tf_op jit(solution)/shard_map/attend/pallas_call | solution.py:327
  60.2 35.9 %all_to_all.10 = bf16[128,24,128]{2,1,0:T(8,128)(2,1)S(1)} all-to-all(bf16[128,24,128]{2,1,0:T(8,128)(2,1)S(1)} %attend.1), channel_id=1, replica_groups=mesh['seq'=128,'head'=4] {'seq'}, dimensions={0} | all-to-all | bytes 1572864 | tf_op jit(solution)/shard_map/all_to_all | solution.py:352
  96.1 1.7 %restore.1 = (bf16[512,128]{1,0:T(8,128)(2,1)}, bf16[512,128]{1,0:T(8,128)(2,1)}, bf16[512,128]{1,0:T(8,128)(2,1)}) custom-call(bf16[64,2,24,128]{3,2,1,0:T(8,128)(2,1)S(1)} %bitcast.2, s32[1,512]{1,0:T(1,128)S(1)} %get-tuple-element.6.code_ref), custom_call_target="tpu_custom_call" | custom-call | tf_op jit(solution)/shard_map/restore/pallas_call | solution.py:343
  (3 shorter events, 0.0 us)
Async XLA Ops:
  0.6 27.3 %collective-permute-start = (s32[1,512]{1,0:T(1,128)}, s32[1,512]{1,0:T(1,128)S(1)}, u32[]{:S(2)}, u32[]{:S(2)}) collective-permute-start(s32[1,512]{1,0:T(1,128)} %param.8), channel_id=1, source_target_pairs={{0,8},{4,12},{8,16},{12,20},{16,24},{20,28},{24,32},{28,36},{32,40... | collective-permute-start | bytes 6152 | tf_op jit(solution)/shard_map/ppermute | solution.py:357
  8.4 19.5 %copy-start.1 = (s32[1,512]{1,0:T(1,128)S(1)}, s32[1,512]{1,0:T(1,128)}, u32[]{:S(2)}) copy-start(s32[1,512]{1,0:T(1,128)} %param.8) | copy-start | bytes 6148
  8.5 45.0 %all-to-all-start = ((bf16[128,24,128]{2,1,0:T(8,128)(2,1)}), bf16[128,24,128]{2,1,0:T(8,128)(2,1)S(1)}, u32[]{:S(2)}, u32[]{:S(2)}) async-start(bf16[128,24,128]{2,1,0:T(8,128)(2,1)} %bitcast), calls=%async_computation | async-start | bytes 1572864 | tf_op jit(solution)/shard_map/all_to_all | solution.py:352
  27.9 3.6 %collective-permute-start.1 = (s32[2,512]{1,0:T(2,128)S(1)}, s32[2,512]{1,0:T(2,128)S(1)}, u32[]{:S(2)}, u32[]{:S(2)}) collective-permute-start(s32[2,512]{1,0:T(2,128)S(1)} %pad_add_fusion.1), channel_id=1, source_target_pairs={{0,4},{4,0},{8,12},{12,8},{16,20},{20,16},{24,28},{28,24},{32,36},... | collective-permute-start | bytes 12296 | tf_op jit(solution)/shard_map/ppermute | solution.py:359
  32.8 0.6 copy-start

commit v3 on v2

--- a/solution.py
+++ b/solution.py
@@ -152,12 +152,9 @@
     return high, (x - high.astype(F32)).astype(BF16)
 
 
-def attend_kernel(arr_ref, table_hbm, out_ref, give_ref, rows_ref, sem):
+def attend_kernel(arr_ref, rows_ref, out_hbm, give_ref, out_ref, sems):
     n, half, group = BLOCK, BLOCK // 2, 8 * PEERS
-    fetch = pltpu.make_async_copy(table_hbm, rows_ref, sem)
-    fetch.start()
     part_z, part_a, part_b, part_g = tiles_of(arr_ref[...].astype(F32))
-    fetch.wait()
     reach = 3 * group // 4
 
     def take(i, part):
@@ -173,6 +170,8 @@
             axis=1,
         )
 
+    give_ref[:, reach:, :half] = jnp.zeros((3, group - reach, half), BF16)
+    give_ref[:, : group - reach, half:] = jnp.zeros((3, group - reach, half), BF16)
     x_z = take(0, part_z)
     x_a = take(1, jnp.concatenate([part_a, part_g], axis=1))
     x_b = take(2, jnp.concatenate([part_b, part_g], axis=1))
@@ -195,30 +194,52 @@
 
     block_z, block_a, block_b = [block_of(x) for x in (x_z, x_a, x_b)]
 
+    first, last = slice(0, half), slice(half, n)
+    row, col = iota((half, half), 0), iota((half, half), 1)
+
+    def low_high(x):
+        return x[:half], x[half:]
+
+    def late(x, y):
+        return jnp.concatenate([x[:, first], x[:, last] + y], axis=1)
+
     def item(prior, own, grads, prior_pos, own_pos):
+        q = own["qb"]
         pos = jnp.concatenate([column(own_pos)] * (n // 128), axis=1)
-        s_prior = tn(own["qb"], prior["qb"]) * prior["scale"]
-        s_prior = jnp.where(prior_pos.astype(F32) < pos, s_prior, masked_score)
-        s_own = tn(own["qb"], own["qb"]) * own["scale"]
-        row, col = iota((n, n), 0), iota((n, n), 1)
-        s_own = jnp.where(col < row, s_own, jnp.where(col == row, self_score, masked_score))
-        top = jnp.maximum(
-            jnp.max(s_prior, axis=1, keepdims=True), jnp.max(s_own, axis=1, keepdims=True)
-        )
-        p_prior = jnp.exp2(s_prior - top)
-        p_own = jnp.exp2(s_own - top)
-        pb_prior, pb_own = p_prior.astype(BF16), p_own.astype(BF16)
-        summed = nt(prior["vb"], pb_prior) + nt(own["vb"], pb_own)
+        s0 = tn(q, prior["qb"]) * prior["scale"]
+        s0 = jnp.where(prior_pos.astype(F32) < pos, s0, masked_score)
+        s1 = tn(q, own["qb"][:, first]) * own["scale"][:, first]
+        s2 = tn(q[:, last], own["qb"][:, last]) * own["scale"][:, last]
+
+        def triangle(s):
+            return jnp.where(col < row, s, jnp.where(col == row, self_score, masked_score))
+
+        s1 = jnp.concatenate([triangle(s1[:half]), s1[half:]], axis=0)
+        s2 = triangle(s2)
+        top0, top1, top2 = (jnp.max(s, axis=1, keepdims=True) for s in (s0, s1, s2))
+        top_low, top_high = low_high(jnp.maximum(top0, top1))
+        top_high = jnp.maximum(top_high, top2)
+        top = jnp.concatenate([top_low, top_high], axis=0)
+        p0, p1, p2 = jnp.exp2(s0 - top), jnp.exp2(s1 - top), jnp.exp2(s2 - top_high)
+        b0, b1, b2 = p0.astype(BF16), p1.astype(BF16), p2.astype(BF16)
+        v0, v1, v2 = prior["vb"], own["vb"][:, first], own["vb"][:, last]
+        summed = late(nt(v0, b0) + nt(v1, b1), nt(v2, b2))
         inverse = 1.0 / summed[h : h + 1]
         out = (summed[:h] * inverse).astype(BF16)
         grad = (grads * inverse).astype(BF16)
         delta = jnp.sum(grad.astype(F32) * out.astype(F32), axis=0, keepdims=True)
         left = jnp.concatenate([grad, *two_terms(-delta), pad], axis=0)
-        ds_prior = (p_prior * tn(left, prior["vb"])).astype(BF16)
-        ds_own = (p_own * tn(left, own["vb"])).astype(BF16)
-        dq = nt(prior["key"], ds_prior) + nt(own["key"], ds_own)
-        sums_prior = (mm(own["qb"], ds_prior), mm(grad, pb_prior))
-        sums_own = (mm(own["qb"], ds_own), mm(grad, pb_own))
+        d0 = (p0 * tn(left, v0)).astype(BF16)
+        d1 = (p1 * tn(left, v1)).astype(BF16)
+        d2 = (p2 * tn(left[:, last], v2)).astype(BF16)
+        dq = late(
+            nt(prior["key"], d0) + nt(own["key"][:, first], d1), nt(own["key"][:, last], d2)
+        )
+        sums_prior = (mm(q, d0), mm(grad, b0))
+        sums_own = tuple(
+            jnp.concatenate([mm(x, lo), mm(x[:, last], hi)], axis=1)
+            for x, lo, hi in ((q, d1, d2), (grad, b1, b2))
+        )
         return out, dq, sums_prior, sums_own
 
     pos_z, pos_a, pos_b = rows_ref[0:1], rows_ref[1:2], rows_ref[2:3]
@@ -235,22 +256,31 @@
             dk = dk + query_grad
         return [dk.astype(BF16), dv.astype(BF16)]
 
-    def send(i, pieces):
-        turned = jnp.concatenate(pieces, axis=0)
-        sent = []
-        for t, (lo, hi) in enumerate([(0, half), (0, n), (0, n), (half, n)]):
-            sent.append(nt(give_ref[i, t * group // 4 : (t + 1) * group // 4, lo:hi], turned[:, lo:hi]))
-        return jnp.concatenate(sent, axis=0)
-
-    give_ref[:, reach:, :half] = jnp.zeros((3, group - reach, half), BF16)
-    give_ref[:, : group - reach, half:] = jnp.zeros((3, group - reach, half), BF16)
     none = jnp.zeros((h, n), BF16)
-    s_z = send(0, result(block_z, sums_z, None)).reshape(PEERS, 8, 128)
-    s_a = send(1, [*result(block_a, sums_a, dq_a), out_a, none])
-    s_b = send(2, [*result(block_b, sums_b, dq_b), none, out_b])
-    mixed = (s_a[:, 128:] + s_b[:, 128:]).reshape(PEERS, 8, 128)
-    s_a, s_b = (s[:, :128].reshape(PEERS, 8, 128) for s in (s_a, s_b))
-    out_ref[...] = rows_of([s_z, s_a, s_b], mixed)
+    turned = [
+        jnp.concatenate(pieces, axis=0)
+        for pieces in (
+            result(block_z, sums_z, None),
+            [*result(block_a, sums_a, dq_a), out_a, none],
+            [*result(block_b, sums_b, dq_b), none, out_b],
+        )
+    ]
+    sends = []
+    for t, used in enumerate((first, slice(0, n), slice(0, n), last)):
+        places = slice(t * group // 4, (t + 1) * group // 4)
+        peers = slice(t * PEERS // 4, (t + 1) * PEERS // 4)
+        s_z, s_a, s_b = (
+            nt(give_ref[i, places, used], x[:, used]).reshape(PEERS // 4, 8, x.shape[0])
+            for i, x in enumerate(turned)
+        )
+        mixed = s_a[:, :, 128:] + s_b[:, :, 128:]
+        out_ref[peers] = rows_of([s_z, s_a[:, :, :128], s_b[:, :, :128]], mixed)
+        sends.append(
+            pltpu.make_async_copy(out_ref.at[peers], out_hbm.at[peers], sems.at[t])
+        )
+        sends[-1].start()
+    for copy in sends:
+        copy.wait()
 
 
 def restore_kernel(ret_ref, code_ref, att_ref, dqk_ref, dv_ref):
@@ -285,6 +315,10 @@
     dv_ref[...] = jnp.concatenate([grads[:, h : 2 * h], grads[:, 3 * h :]], axis=1)
 
 
+hbm = pl.BlockSpec(memory_space=pltpu.HBM)
+vmem = pl.BlockSpec(memory_space=pltpu.VMEM)
+
+
 def struct(shape, dtype):
     return jax.ShapeDtypeStruct(shape, dtype)
 
@@ -295,6 +329,10 @@
 
 def in_hbm(x):
     return pltpu.with_memory_space_constraint(x, pltpu.HBM)
+
+
+hbm = pl.BlockSpec(memory_space=pltpu.HBM)
+vmem = pl.BlockSpec(memory_space=pltpu.VMEM)
 
 
 def pack(slots, q, v, g):
@@ -324,18 +362,20 @@
 
 
 def attend(arrived, table):
+    shape = (PEERS, ROWS, 128)
     return pl.pallas_call(
         attend_kernel,
-        in_specs=[pl.BlockSpec(memory_space=pltpu.VMEM), pl.BlockSpec(memory_space=pltpu.HBM)],
-        out_shape=struct((PEERS, ROWS, 128), BF16),
+        in_specs=[vmem, vmem],
+        out_specs=hbm,
+        out_shape=struct(shape, BF16),
         scratch_shapes=[
             pltpu.VMEM((3, 8 * PEERS, BLOCK), BF16),
-            pltpu.VMEM((8, BLOCK), I32),
-            pltpu.SemaphoreType.DMA(()),
+            pltpu.VMEM(shape, BF16),
+            pltpu.SemaphoreType.DMA((4,)),
         ],
         compiler_params=params(40),
         name="attend",
-    )(arrived, in_hbm(table))
+    )(arrived, table)
 
 
 def restore(returned, code):

time: 98.2 us -> 98.6 us (level)
  no operation moved by 1% of the time
where the time goes in v3:
time: 98.6 us; the launch traced here: 98.3 us
  blocking collectives  35.9 us (36%)
  starting transfers between devices  27.1 us (27%)
  waiting for transfers between devices  21.4 us (22%)
  Pallas kernels  13.2 us (13%)
    all_to_all x1, blocking collectives, exchange(): lax.all_to_all(message, 'seq', split_axis=0, concat_axis=0, tiled=True)  35.9 us
    all_to_all x1, waiting for transfers between devices, exchange(): lax.all_to_all(message, 'seq', split_axis=0, concat_axis=0, tiled=True)  20.6 us
    all_to_all x1, starting transfers between devices, exchange(): lax.all_to_all(message, 'seq', split_axis=0, concat_axis=0, tiled=True)  19.4 us
    pallas_call x1, Pallas kernels, attend(): pl.pallas_call(attend_kernel, in_specs=[vmem, vmem], out_specs=hbm, out_s...  7.32 us
    ppermute x1, starting transfers between devices, per_device(): lax.ppermute(bucket_order, 'seq', [(i, (i + 2) % PEERS) for i in peers])  4.83 us
    pallas_call x1, Pallas kernels, pack(): pl.pallas_call(pack_kernel, in_specs=[pl.BlockSpec(memory_space=pltpu.HBM...  2.97 us
    ppermute x1, starting transfers between devices, per_device(): other = lax.ppermute(held, 'seq', [(i, i ^ 1) for i in peers])  2.8 us
  transfers between devices with their start and end apart: 3, of which 2 were waited for; matrix products, arithmetic and copies ran while one was open for 0% of the time, Pallas kernels for 4%

profile of v3, /device:TPU:1, one launch (start us, length us, event | category | flops | bytes accessed | tf_op | source)
XLA Modules:
  0.0 98.3 jit_solution(11485328953671706929)
XLA Ops:
  0.6 4.8 %collective-permute-start = (s32[1,512]{1,0:T(1,128)}, s32[1,512]{1,0:T(1,128)S(1)}, u32[]{:S(2)}, u32[]{:S(2)}) collective-permute-start(s32[1,512]{1,0:T(1,128)} %param.8), channel_id=1, source_target_pairs={{0,8},{4,12},{8,16},{12,20},{16,24},{20,28},{24,32},{28,36},{32,40... | collective-permute-start | bytes 6152 | tf_op jit(solution)/shard_map/ppermute | solution.py:397
  5.5 3.0 %pack.1 = (bf16[64,2,24,128]{3,2,1,0:T(8,128)(2,1)}, s32[1,512]{1,0:T(1,128)S(1)}) custom-call(s32[1,512]{1,0:T(1,128)} %slot_hbm.1, bf16[512,128]{1,0:T(8,128)(2,1)} %q_hbm.1, bf16[512,128]{1,0:T(8,128)(2,1)} %v_hbm.1, bf16[512,128]{1,0:T(8,128)(2,1)} %g_hbm.1), custom_call_target="tpu_custom_call" | custom-call | tf_op jit(solution)/shard_map/pack/pallas_call | solution.py:340
  8.5 0.0 copy-start
  8.5 19.4 %all-to-all-start = ((bf16[128,24,128]{2,1,0:T(8,128)(2,1)}), bf16[128,24,128]{2,1,0:T(8,128)(2,1)S(1)}, u32[]{:S(2)}, u32[]{:S(2)}) async-start(bf16[128,24,128]{2,1,0:T(8,128)(2,1)} %bitcast), calls=%async_computation | async-start | bytes 1572864 | tf_op jit(solution)/shard_map/all_to_all | solution.py:392
  27.9 0.0 collective-permute-done
  27.9 0.0 copy-done
  27.9 2.8 %collective-permute-start.1 = (s32[2,512]{1,0:T(2,128)S(1)}, s32[2,512]{1,0:T(2,128)S(1)}, u32[]{:S(2)}, u32[]{:S(2)}) collective-permute-start(s32[2,512]{1,0:T(2,128)S(1)} %pad_add_fusion.1), channel_id=1, source_target_pairs={{0,4},{4,0},{8,12},{12,8},{16,20},{20,16},{24,28},{28,24},{32,36},... | collective-permute-start | bytes 12296 | tf_op jit(solution)/shard_map/ppermute | solution.py:399
  30.8 0.8 collective-permute-done.1
  31.6 1.3 %meta.1.rows_ref = s32[8,512]{1,0:T(8,128)S(1)} custom-call(s32[3,512]{1,0:T(4,128)S(1)} %pad_add_fusion.orders_ref, s32[1,512]{1,0:T(1,128)S(1)} %get-tuple-element.6.code_ref), custom_call_target="tpu_custom_call" | custom-call | flops 12000000000 | bytes 32768 | tf_op jit(solution)/shard_map/meta/pallas_call | solution.py:353
  32.8 20.6 %all-to-all-done.arr_ref = bf16[128,24,128]{2,1,0:T(8,128)(2,1)S(1)} async-done(((bf16[128,24,128]{2,1,0:T(8,128)(2,1)}), bf16[128,24,128]{2,1,0:T(8,128)(2,1)S(1)}, u32[]{:S(2)}, u32[]{:S(2)}) %all-to-all-start) | async-done | bytes 786464 | tf_op jit(solution)/shard_map/all_to_all | solution.py:392
  53.4 7.3 %attend.1 = bf16[128,24,128]{2,1,0:T(8,128)(2,1)S(1)} custom-call(bf16[128,24,128]{2,1,0:T(8,128)(2,1)S(1)} %all-to-all-done.arr_ref, s32[8,512]{1,0:T(8,128)S(1)} %meta.1.rows_ref), custom_call_target="tpu_custom_call" | custom-call | tf_op jit(solution)/shard_map/attend/pallas_call | solution.py:366
  60.8 35.9 %all_to_all.10 = bf16[128,24,128]{2,1,0:T(8,128)(2,1)S(1)} all-to-all(bf16[128,24,128]{2,1,0:T(8,128)(2,1)S(1)} %attend.1), channel_id=1, replica_groups=mesh['seq'=128,'head'=4] {'seq'}, dimensions={0} | all-to-all | bytes 1572864 | tf_op jit(solution)/shard_map/all_to_all | solution.py:392
  96.6 1.7 %restore.1 = (bf16[512,128]{1,0:T(8,128)(2,1)}, bf16[512,128]{1,0:T(8,128)(2,1)}, bf16[512,128]{1,0:T(8,128)(2,1)}) custom-call(bf16[64,2,24,128]{3,2,1,0:T(8,128)(2,1)S(1)} %bitcast.2, s32[1,512]{1,0:T(1,128)S(1)} %get-tuple-element.6.code_ref), custom_call_target="tpu_custom_call" | custom-call | tf_op jit(solution)/shard_map/restore/pallas_call | solution.py:383
  (3 shorter events, 0.0 us)
Async XLA Ops:
  0.6 27.3 %collective-permute-start = (s32[1,512]{1,0:T(1,128)}, s32[1,512]{1,0:T(1,128)S(1)}, u32[]{:S(2)}, u32[]{:S(2)}) collective-permute-start(s32[1,512]{1,0:T(1,128)} %param.8), channel_id=1, source_target_pairs={{0,8},{4,12},{8,16},{12,20},{16,24},{20,28},{24,32},{28,36},{32,40... | collective-permute-start | bytes 6152 | tf_op jit(solution)/shard_map/ppermute | solution.py:397
  8.5 19.5 %copy-start = (s32[1,512]{1,0:T(1,128)S(1)}, s32[1,512]{1,0:T(1,128)}, u32[]{:S(2)}) copy-start(s32[1,512]{1,0:T(1,128)} %param.8) | copy-start | bytes 6148
  8.5 45.0 %all-to-all-start = ((bf16[128,24,128]{2,1,0:T(8,128)(2,1)}), bf16[128,24,128]{2,1,0:T(8,128)(2,1)S(1)}, u32[]{:S(2)}, u32[]{:S(2)}) async-start(bf16[128,24,128]{2,1,0:T(8,128)(2,1)} %bitcast), calls=%async_computation | async-start | bytes 1572864 | tf_op jit(solution)/shard_map/all_to_all | solution.py:392
  27.9 3.6 %collective-permute-start.1 = (s32[2,512]{1,0:T(2,128)S(1)}, s32[2,512]{1,0:T(2,128)S(1)}, u32[]{:S(2)}, u32[]{:S(2)}) collective-permute-start(s32[2,512]{1,0:T(2,128)S(1)} %pad_add_fusion.1), channel_id=1, source_target_pairs={{0,4},{4,0},{8,12},{12,8},{16,20},{20,16},{24,28},{28,24},{32,36},... | collective-permute-start | bytes 12296 | tf_op jit(solution)/shard_map/ppermute | solution.py:399

commit v4 on v3

--- a/solution.py
+++ b/solution.py
@@ -152,7 +152,7 @@
     return high, (x - high.astype(F32)).astype(BF16)
 
 
-def attend_kernel(arr_ref, rows_ref, out_hbm, give_ref, out_ref, sems):
+def attend_kernel(arr_ref, rows_ref, out_ref, give_ref):
     n, half, group = BLOCK, BLOCK // 2, 8 * PEERS
     part_z, part_a, part_b, part_g = tiles_of(arr_ref[...].astype(F32))
     reach = 3 * group // 4
@@ -265,7 +265,6 @@
             [*result(block_b, sums_b, dq_b), none, out_b],
         )
     ]
-    sends = []
     for t, used in enumerate((first, slice(0, n), slice(0, n), last)):
         places = slice(t * group // 4, (t + 1) * group // 4)
         peers = slice(t * PEERS // 4, (t + 1) * PEERS // 4)
@@ -275,12 +274,6 @@
         )
         mixed = s_a[:, :, 128:] + s_b[:, :, 128:]
         out_ref[peers] = rows_of([s_z, s_a[:, :, :128], s_b[:, :, :128]], mixed)
-        sends.append(
-            pltpu.make_async_copy(out_ref.at[peers], out_hbm.at[peers], sems.at[t])
-        )
-        sends[-1].start()
-    for copy in sends:
-        copy.wait()
 
 
 def restore_kernel(ret_ref, code_ref, att_ref, dqk_ref, dv_ref):
@@ -315,10 +308,6 @@
     dv_ref[...] = jnp.concatenate([grads[:, h : 2 * h], grads[:, 3 * h :]], axis=1)
 
 
-hbm = pl.BlockSpec(memory_space=pltpu.HBM)
-vmem = pl.BlockSpec(memory_space=pltpu.VMEM)
-
-
 def struct(shape, dtype):
     return jax.ShapeDtypeStruct(shape, dtype)
 
@@ -329,10 +318,6 @@
 
 def in_hbm(x):
     return pltpu.with_memory_space_constraint(x, pltpu.HBM)
-
-
-hbm = pl.BlockSpec(memory_space=pltpu.HBM)
-vmem = pl.BlockSpec(memory_space=pltpu.VMEM)
 
 
 def pack(slots, q, v, g):
@@ -365,13 +350,9 @@
     shape = (PEERS, ROWS, 128)
     return pl.pallas_call(
         attend_kernel,
-        in_specs=[vmem, vmem],
-        out_specs=hbm,
         out_shape=struct(shape, BF16),
         scratch_shapes=[
             pltpu.VMEM((3, 8 * PEERS, BLOCK), BF16),
-            pltpu.VMEM(shape, BF16),
-            pltpu.SemaphoreType.DMA((4,)),
         ],
         compiler_params=params(40),
         name="attend",

time: 98.6 us -> 97 us (0.984)
  Pallas kernels: 13.2 us -> 11.7 us
    pallas_call x1, Pallas kernels: 7.32 us -> 5.77 us  [attend(): pl.pallas_call(attend_kernel, out_shape=struct(shape, BF16), scratch_shap...]
where the time goes in v4:
time: 97 us; the launch traced here: 96.8 us
  blocking collectives  35.9 us (37%)
  starting transfers between devices  27.1 us (28%)
  waiting for transfers between devices  21.4 us (22%)
  Pallas kernels  11.7 us (12%)
    all_to_all x1, blocking collectives, exchange(): lax.all_to_all(message, 'seq', split_axis=0, concat_axis=0, tiled=True)  35.9 us
    all_to_all x1, waiting for transfers between devices, exchange(): lax.all_to_all(message, 'seq', split_axis=0, concat_axis=0, tiled=True)  20.6 us
    all_to_all x1, starting transfers between devices, exchange(): lax.all_to_all(message, 'seq', split_axis=0, concat_axis=0, tiled=True)  19.4 us
    pallas_call x1, Pallas kernels, attend(): pl.pallas_call(attend_kernel, out_shape=struct(shape, BF16), scratch_shap...  5.77 us
    ppermute x1, starting transfers between devices, per_device(): lax.ppermute(bucket_order, 'seq', [(i, (i + 2) % PEERS) for i in peers])  4.83 us
    pallas_call x1, Pallas kernels, pack(): pl.pallas_call(pack_kernel, in_specs=[pl.BlockSpec(memory_space=pltpu.HBM...  2.97 us
    ppermute x1, starting transfers between devices, per_device(): other = lax.ppermute(held, 'seq', [(i, i ^ 1) for i in peers])  2.8 us
  transfers between devices with their start and end apart: 3, of which 2 were waited for; matrix products, arithmetic and copies ran while one was open for 0% of the time, Pallas kernels for 4%

profile of v4, /device:TPU:1, one launch (start us, length us, event | category | flops | bytes accessed | tf_op | source)
XLA Modules:
  0.0 96.8 jit_solution(14333632631036325317)
XLA Ops:
  0.6 4.8 %collective-permute-start = (s32[1,512]{1,0:T(1,128)}, s32[1,512]{1,0:T(1,128)S(1)}, u32[]{:S(2)}, u32[]{:S(2)}) collective-permute-start(s32[1,512]{1,0:T(1,128)} %param.8), channel_id=1, source_target_pairs={{0,8},{4,12},{8,16},{12,20},{16,24},{20,28},{24,32},{28,36},{32,40... | collective-permute-start | bytes 6152 | tf_op jit(solution)/shard_map/ppermute | solution.py:378
  5.5 3.0 %pack.1 = (bf16[64,2,24,128]{3,2,1,0:T(8,128)(2,1)}, s32[1,512]{1,0:T(1,128)S(1)}) custom-call(s32[1,512]{1,0:T(1,128)} %slot_hbm.1, bf16[512,128]{1,0:T(8,128)(2,1)} %q_hbm.1, bf16[512,128]{1,0:T(8,128)(2,1)} %v_hbm.1, bf16[512,128]{1,0:T(8,128)(2,1)} %g_hbm.1), custom_call_target="tpu_custom_call" | custom-call | tf_op jit(solution)/shard_map/pack/pallas_call | solution.py:325
  8.5 0.0 copy-start
  8.5 19.4 %all-to-all-start = ((bf16[128,24,128]{2,1,0:T(8,128)(2,1)}), bf16[128,24,128]{2,1,0:T(8,128)(2,1)S(1)}, u32[]{:S(2)}, u32[]{:S(2)}) async-start(bf16[128,24,128]{2,1,0:T(8,128)(2,1)} %bitcast), calls=%async_computation | async-start | bytes 1572864 | tf_op jit(solution)/shard_map/all_to_all | solution.py:373
  27.9 0.0 collective-permute-done
  27.9 0.0 copy-done
  27.9 2.8 %collective-permute-start.1 = (s32[2,512]{1,0:T(2,128)S(1)}, s32[2,512]{1,0:T(2,128)S(1)}, u32[]{:S(2)}, u32[]{:S(2)}) collective-permute-start(s32[2,512]{1,0:T(2,128)S(1)} %pad_add_fusion.1), channel_id=1, source_target_pairs={{0,4},{4,0},{8,12},{12,8},{16,20},{20,16},{24,28},{28,24},{32,36},... | collective-permute-start | bytes 12296 | tf_op jit(solution)/shard_map/ppermute | solution.py:380
  30.8 0.8 collective-permute-done.1
  31.6 1.3 %meta.1.rows_ref = s32[8,512]{1,0:T(8,128)S(1)} custom-call(s32[3,512]{1,0:T(4,128)S(1)} %pad_add_fusion.orders_ref, s32[1,512]{1,0:T(1,128)S(1)} %get-tuple-element.6.code_ref), custom_call_target="tpu_custom_call" | custom-call | flops 12000000000 | bytes 32768 | tf_op jit(solution)/shard_map/meta/pallas_call | solution.py:338
  32.8 20.6 %all-to-all-done.arr_ref = bf16[128,24,128]{2,1,0:T(8,128)(2,1)S(1)} async-done(((bf16[128,24,128]{2,1,0:T(8,128)(2,1)}), bf16[128,24,128]{2,1,0:T(8,128)(2,1)S(1)}, u32[]{:S(2)}, u32[]{:S(2)}) %all-to-all-start) | async-done | bytes 786464 | tf_op jit(solution)/shard_map/all_to_all | solution.py:373
  53.4 5.8 %attend.1 = bf16[128,24,128]{2,1,0:T(8,128)(2,1)S(1)} custom-call(bf16[128,24,128]{2,1,0:T(8,128)(2,1)S(1)} %all-to-all-done.arr_ref, s32[8,512]{1,0:T(8,128)S(1)} %meta.1.rows_ref), custom_call_target="tpu_custom_call" | custom-call | tf_op jit(solution)/shard_map/attend/pallas_call | solution.py:351
  59.2 35.9 %all_to_all.10 = bf16[128,24,128]{2,1,0:T(8,128)(2,1)S(1)} all-to-all(bf16[128,24,128]{2,1,0:T(8,128)(2,1)S(1)} %attend.1), channel_id=1, replica_groups=mesh['seq'=128,'head'=4] {'seq'}, dimensions={0} | all-to-all | bytes 1572864 | tf_op jit(solution)/shard_map/all_to_all | solution.py:373
  95.1 1.7 %restore.1 = (bf16[512,128]{1,0:T(8,128)(2,1)}, bf16[512,128]{1,0:T(8,128)(2,1)}, bf16[512,128]{1,0:T(8,128)(2,1)}) custom-call(bf16[64,2,24,128]{3,2,1,0:T(8,128)(2,1)S(1)} %bitcast.2, s32[1,512]{1,0:T(1,128)S(1)} %get-tuple-element.6.code_ref), custom_call_target="tpu_custom_call" | custom-call | tf_op jit(solution)/shard_map/restore/pallas_call | solution.py:364
  (3 shorter events, 0.0 us)
Async XLA Ops:
  0.6 27.3 %collective-permute-start = (s32[1,512]{1,0:T(1,128)}, s32[1,512]{1,0:T(1,128)S(1)}, u32[]{:S(2)}, u32[]{:S(2)}) collective-permute-start(s32[1,512]{1,0:T(1,128)} %param.8), channel_id=1, source_target_pairs={{0,8},{4,12},{8,16},{12,20},{16,24},{20,28},{24,32},{28,36},{32,40... | collective-permute-start | bytes 6152 | tf_op jit(solution)/shard_map/ppermute | solution.py:378
  8.5 19.5 %copy-start = (s32[1,512]{1,0:T(1,128)S(1)}, s32[1,512]{1,0:T(1,128)}, u32[]{:S(2)}) copy-start(s32[1,512]{1,0:T(1,128)} %param.8) | copy-start | bytes 6148
  8.5 45.0 %all-to-all-start = ((bf16[128,24,128]{2,1,0:T(8,128)(2,1)}), bf16[128,24,128]{2,1,0:T(8,128)(2,1)S(1)}, u32[]{:S(2)}, u32[]{:S(2)}) async-start(bf16[128,24,128]{2,1,0:T(8,128)(2,1)} %bitcast), calls=%async_computation | async-start | bytes 1572864 | tf_op jit(solution)/shard_map/all_to_all | solution.py:373
  27.9 3.6 %collective-permute-start.1 = (s32[2,512]{1,0:T(2,128)S(1)}, s32[2,512]{1,0:T(2,128)S(1)}, u32[]{:S(2)}, u32[]{:S(2)}) collective-permute-start(s32[2,512]{1,0:T(2,128)S(1)} %pad_add_fusion.1), channel_id=1, source_target_pairs={{0,4},{4,0},{8,12},{12,8},{16,20},{20,16},{24,28},{28,24},{32,36},... | collective-permute-start | bytes 12296 | tf_op jit(solution)/shard_map/ppermute | solution.py:380

commit v5 on v4

--- a/solution.py
+++ b/solution.py
@@ -210,6 +210,7 @@
         s0 = jnp.where(prior_pos.astype(F32) < pos, s0, masked_score)
         s1 = tn(q, own["qb"][:, first]) * own["scale"][:, first]
         s2 = tn(q[:, last], own["qb"][:, last]) * own["scale"][:, last]
+        yield
 
         def triangle(s):
             return jnp.where(col < row, s, jnp.where(col == row, self_score, masked_score))
@@ -222,6 +223,7 @@
         top = jnp.concatenate([top_low, top_high], axis=0)
         p0, p1, p2 = jnp.exp2(s0 - top), jnp.exp2(s1 - top), jnp.exp2(s2 - top_high)
         b0, b1, b2 = p0.astype(BF16), p1.astype(BF16), p2.astype(BF16)
+        yield
         v0, v1, v2 = prior["vb"], own["vb"][:, first], own["vb"][:, last]
         summed = late(nt(v0, b0) + nt(v1, b1), nt(v2, b2))
         inverse = 1.0 / summed[h : h + 1]
@@ -229,9 +231,11 @@
         grad = (grads * inverse).astype(BF16)
         delta = jnp.sum(grad.astype(F32) * out.astype(F32), axis=0, keepdims=True)
         left = jnp.concatenate([grad, *two_terms(-delta), pad], axis=0)
+        yield
         d0 = (p0 * tn(left, v0)).astype(BF16)
         d1 = (p1 * tn(left, v1)).astype(BF16)
         d2 = (p2 * tn(left[:, last], v2)).astype(BF16)
+        yield
         dq = late(
             nt(prior["key"], d0) + nt(own["key"][:, first], d1), nt(own["key"][:, last], d2)
         )
@@ -240,11 +244,18 @@
             jnp.concatenate([mm(x, lo), mm(x[:, last], hi)], axis=1)
             for x, lo, hi in ((q, d1, d2), (grad, b1, b2))
         )
-        return out, dq, sums_prior, sums_own
+        yield out, dq, sums_prior, sums_own
 
     pos_z, pos_a, pos_b = rows_ref[0:1], rows_ref[1:2], rows_ref[2:3]
-    out_a, dq_a, sums_z, sums_a = item(block_z, block_a, g_a, pos_z, pos_a)
-    out_b, dq_b, more_a, sums_b = item(block_a, block_b, g_b, pos_a, pos_b)
+    items = [
+        item(block_z, block_a, g_a, pos_z, pos_a),
+        item(block_a, block_b, g_b, pos_a, pos_b),
+    ]
+    ends = {}
+    for i in (0, 0, 1, 0, 1, 0, 1, 0, 1, 1):
+        ends[i] = next(items[i])
+    out_a, dq_a, sums_z, sums_a = ends[0]
+    out_b, dq_b, more_a, sums_b = ends[1]
     sums_a = (sums_a[0] + more_a[0], sums_a[1] + more_a[1])
 
     def result(block, sums, query_grad):

time: 97 us -> 96.4 us (level)
  no operation moved by 1% of the time
where the time goes in v5:
time: 96.4 us; the launch traced here: 96.1 us
  blocking collectives  35.9 us (37%)
  starting transfers between devices  27.1 us (28%)
  waiting for transfers between devices  21.4 us (22%)
  Pallas kernels  11.1 us (12%)
    all_to_all x1, blocking collectives, exchange(): lax.all_to_all(message, 'seq', split_axis=0, concat_axis=0, tiled=True)  35.9 us
    all_to_all x1, waiting for transfers between devices, exchange(): lax.all_to_all(message, 'seq', split_axis=0, concat_axis=0, tiled=True)  20.6 us
    all_to_all x1, starting transfers between devices, exchange(): lax.all_to_all(message, 'seq', split_axis=0, concat_axis=0, tiled=True)  19.4 us
    pallas_call x1, Pallas kernels, attend(): pl.pallas_call(attend_kernel, out_shape=struct(shape, BF16), scratch_shap...  5.15 us
    ppermute x1, starting transfers between devices, per_device(): lax.ppermute(bucket_order, 'seq', [(i, (i + 2) % PEERS) for i in peers])  4.83 us
    pallas_call x1, Pallas kernels, pack(): pl.pallas_call(pack_kernel, in_specs=[pl.BlockSpec(memory_space=pltpu.HBM...  2.97 us
    ppermute x1, starting transfers between devices, per_device(): other = lax.ppermute(held, 'seq', [(i, i ^ 1) for i in peers])  2.8 us
  transfers between devices with their start and end apart: 3, of which 2 were waited for; matrix products, arithmetic and copies ran while one was open for 0% of the time, Pallas kernels for 4%

profile of v5, /device:TPU:1, one launch (start us, length us, event | category | flops | bytes accessed | tf_op | source)
XLA Modules:
  0.0 96.1 jit_solution(7631709606136089407)
XLA Ops:
  0.6 4.8 %collective-permute-start = (s32[1,512]{1,0:T(1,128)}, s32[1,512]{1,0:T(1,128)S(1)}, u32[]{:S(2)}, u32[]{:S(2)}) collective-permute-start(s32[1,512]{1,0:T(1,128)} %param.8), channel_id=1, source_target_pairs={{0,8},{4,12},{8,16},{12,20},{16,24},{20,28},{24,32},{28,36},{32,40... | collective-permute-start | bytes 6152 | tf_op jit(solution)/shard_map/ppermute | solution.py:389
  5.5 3.0 %pack.1 = (bf16[64,2,24,128]{3,2,1,0:T(8,128)(2,1)}, s32[1,512]{1,0:T(1,128)S(1)}) custom-call(s32[1,512]{1,0:T(1,128)} %slot_hbm.1, bf16[512,128]{1,0:T(8,128)(2,1)} %q_hbm.1, bf16[512,128]{1,0:T(8,128)(2,1)} %v_hbm.1, bf16[512,128]{1,0:T(8,128)(2,1)} %g_hbm.1), custom_call_target="tpu_custom_call" | custom-call | tf_op jit(solution)/shard_map/pack/pallas_call | solution.py:336
  8.5 0.0 copy-start
  8.5 19.4 %all-to-all-start = ((bf16[128,24,128]{2,1,0:T(8,128)(2,1)}), bf16[128,24,128]{2,1,0:T(8,128)(2,1)S(1)}, u32[]{:S(2)}, u32[]{:S(2)}) async-start(bf16[128,24,128]{2,1,0:T(8,128)(2,1)} %bitcast), calls=%async_computation | async-start | bytes 1572864 | tf_op jit(solution)/shard_map/all_to_all | solution.py:384
  27.9 0.0 collective-permute-done
  27.9 0.0 copy-done
  27.9 2.8 %collective-permute-start.1 = (s32[2,512]{1,0:T(2,128)S(1)}, s32[2,512]{1,0:T(2,128)S(1)}, u32[]{:S(2)}, u32[]{:S(2)}) collective-permute-start(s32[2,512]{1,0:T(2,128)S(1)} %pad_add_fusion.1), channel_id=1, source_target_pairs={{0,4},{4,0},{8,12},{12,8},{16,20},{20,16},{24,28},{28,24},{32,36},... | collective-permute-start | bytes 12296 | tf_op jit(solution)/shard_map/ppermute | solution.py:391
  30.8 0.8 collective-permute-done.1
  31.6 1.3 %meta.1.rows_ref = s32[8,512]{1,0:T(8,128)S(1)} custom-call(s32[3,512]{1,0:T(4,128)S(1)} %pad_add_fusion.orders_ref, s32[1,512]{1,0:T(1,128)S(1)} %get-tuple-element.6.code_ref), custom_call_target="tpu_custom_call" | custom-call | flops 12000000000 | bytes 32768 | tf_op jit(solution)/shard_map/meta/pallas_call | solution.py:349
  32.8 20.6 %all-to-all-done.arr_ref = bf16[128,24,128]{2,1,0:T(8,128)(2,1)S(1)} async-done(((bf16[128,24,128]{2,1,0:T(8,128)(2,1)}), bf16[128,24,128]{2,1,0:T(8,128)(2,1)S(1)}, u32[]{:S(2)}, u32[]{:S(2)}) %all-to-all-start) | async-done | bytes 786464 | tf_op jit(solution)/shard_map/all_to_all | solution.py:384
  53.4 5.2 %attend.1 = bf16[128,24,128]{2,1,0:T(8,128)(2,1)S(1)} custom-call(bf16[128,24,128]{2,1,0:T(8,128)(2,1)S(1)} %all-to-all-done.arr_ref, s32[8,512]{1,0:T(8,128)S(1)} %meta.1.rows_ref), custom_call_target="tpu_custom_call" | custom-call | tf_op jit(solution)/shard_map/attend/pallas_call | solution.py:362
  58.6 35.9 %all_to_all.10 = bf16[128,24,128]{2,1,0:T(8,128)(2,1)S(1)} all-to-all(bf16[128,24,128]{2,1,0:T(8,128)(2,1)S(1)} %attend.1), channel_id=1, replica_groups=mesh['seq'=128,'head'=4] {'seq'}, dimensions={0} | all-to-all | bytes 1572864 | tf_op jit(solution)/shard_map/all_to_all | solution.py:384
  94.5 1.7 %restore.1 = (bf16[512,128]{1,0:T(8,128)(2,1)}, bf16[512,128]{1,0:T(8,128)(2,1)}, bf16[512,128]{1,0:T(8,128)(2,1)}) custom-call(bf16[64,2,24,128]{3,2,1,0:T(8,128)(2,1)S(1)} %bitcast.2, s32[1,512]{1,0:T(1,128)S(1)} %get-tuple-element.6.code_ref), custom_call_target="tpu_custom_call" | custom-call | tf_op jit(solution)/shard_map/restore/pallas_call | solution.py:375
  (3 shorter events, 0.0 us)
Async XLA Ops:
  0.6 27.3 %collective-permute-start = (s32[1,512]{1,0:T(1,128)}, s32[1,512]{1,0:T(1,128)S(1)}, u32[]{:S(2)}, u32[]{:S(2)}) collective-permute-start(s32[1,512]{1,0:T(1,128)} %param.8), channel_id=1, source_target_pairs={{0,8},{4,12},{8,16},{12,20},{16,24},{20,28},{24,32},{28,36},{32,40... | collective-permute-start | bytes 6152 | tf_op jit(solution)/shard_map/ppermute | solution.py:389
  8.5 19.5 %copy-start = (s32[1,512]{1,0:T(1,128)S(1)}, s32[1,512]{1,0:T(1,128)}, u32[]{:S(2)}) copy-start(s32[1,512]{1,0:T(1,128)} %param.8) | copy-start | bytes 6148
  8.5 45.0 %all-to-all-start = ((bf16[128,24,128]{2,1,0:T(8,128)(2,1)}), bf16[128,24,128]{2,1,0:T(8,128)(2,1)S(1)}, u32[]{:S(2)}, u32[]{:S(2)}) async-start(bf16[128,24,128]{2,1,0:T(8,128)(2,1)} %bitcast), calls=%async_computation | async-start | bytes 1572864 | tf_op jit(solution)/shard_map/all_to_all | solution.py:384
  27.9 3.6 %collective-permute-start.1 = (s32[2,512]{1,0:T(2,128)S(1)}, s32[2,512]{1,0:T(2,128)S(1)}, u32[]{:S(2)}, u32[]{:S(2)}) collective-permute-start(s32[2,512]{1,0:T(2,128)S(1)} %pad_add_fusion.1), channel_id=1, source_target_pairs={{0,4},{4,0},{8,12},{12,8},{16,20},{20,16},{24,28},{28,24},{32,36},... | collective-permute-start | bytes 12296 | tf_op jit(solution)/shard_map/ppermute | solution.py:391

commit v6 on v5

--- a/solution.py
+++ b/solution.py
@@ -170,14 +170,12 @@
             axis=1,
         )
 
-    give_ref[:, reach:, :half] = jnp.zeros((3, group - reach, half), BF16)
-    give_ref[:, : group - reach, half:] = jnp.zeros((3, group - reach, half), BF16)
     x_z = take(0, part_z)
     x_a = take(1, jnp.concatenate([part_a, part_g], axis=1))
     x_b = take(2, jnp.concatenate([part_b, part_g], axis=1))
     h = HEAD_DIM
     g_a, g_b = x_a[2 * h : 3 * h], x_b[3 * h :]
-    pad = jnp.zeros((14, n), BF16)
+    pad = jnp.zeros((14, n), F32)
     ones = jnp.ones((16, n), BF16)
 
     def block_of(x):
@@ -230,7 +228,8 @@
         out = (summed[:h] * inverse).astype(BF16)
         grad = (grads * inverse).astype(BF16)
         delta = jnp.sum(grad.astype(F32) * out.astype(F32), axis=0, keepdims=True)
-        left = jnp.concatenate([grad, *two_terms(-delta), pad], axis=0)
+        terms = [x.astype(F32) for x in (grad, *two_terms(-delta))]
+        left = jnp.concatenate([*terms, pad], axis=0).astype(BF16)
         yield
         d0 = (p0 * tn(left, v0)).astype(BF16)
         d1 = (p1 * tn(left, v1)).astype(BF16)

time: 96.4 us -> 96.4 us (level)
  no operation moved by 1% of the time
where the time goes in v6:
time: 96.4 us; the launch traced here: 96.1 us
  blocking collectives  35.9 us (37%)
  starting transfers between devices  27.1 us (28%)
  waiting for transfers between devices  21.4 us (22%)
  Pallas kernels  11.1 us (12%)
    all_to_all x1, blocking collectives, exchange(): lax.all_to_all(message, 'seq', split_axis=0, concat_axis=0, tiled=True)  35.9 us
    all_to_all x1, waiting for transfers between devices, exchange(): lax.all_to_all(message, 'seq', split_axis=0, concat_axis=0, tiled=True)  20.6 us
    all_to_all x1, starting transfers between devices, exchange(): lax.all_to_all(message, 'seq', split_axis=0, concat_axis=0, tiled=True)  19.4 us
    pallas_call x1, Pallas kernels, attend(): pl.pallas_call(attend_kernel, out_shape=struct(shape, BF16), scratch_shap...  5.14 us
    ppermute x1, starting transfers between devices, per_device(): lax.ppermute(bucket_order, 'seq', [(i, (i + 2) % PEERS) for i in peers])  4.83 us
    pallas_call x1, Pallas kernels, pack(): pl.pallas_call(pack_kernel, in_specs=[pl.BlockSpec(memory_space=pltpu.HBM...  2.97 us
    ppermute x1, starting transfers between devices, per_device(): other = lax.ppermute(held, 'seq', [(i, i ^ 1) for i in peers])  2.8 us
  transfers between devices with their start and end apart: 3, of which 2 were waited for; matrix products, arithmetic and copies ran while one was open for 0% of the time, Pallas kernels for 4%

profile of v6, /device:TPU:1, one launch (start us, length us, event | category | flops | bytes accessed | tf_op | source)
XLA Modules:
  0.0 96.1 jit_solution(14495155058022402248)
XLA Ops:
  0.6 4.8 %collective-permute-start = (s32[1,512]{1,0:T(1,128)}, s32[1,512]{1,0:T(1,128)S(1)}, u32[]{:S(2)}, u32[]{:S(2)}) collective-permute-start(s32[1,512]{1,0:T(1,128)} %param.8), channel_id=1, source_target_pairs={{0,8},{4,12},{8,16},{12,20},{16,24},{20,28},{24,32},{28,36},{32,40... | collective-permute-start | bytes 6152 | tf_op jit(solution)/shard_map/ppermute | solution.py:388
  5.5 3.0 %pack.1 = (bf16[64,2,24,128]{3,2,1,0:T(8,128)(2,1)}, s32[1,512]{1,0:T(1,128)S(1)}) custom-call(s32[1,512]{1,0:T(1,128)} %slot_hbm.1, bf16[512,128]{1,0:T(8,128)(2,1)} %q_hbm.1, bf16[512,128]{1,0:T(8,128)(2,1)} %v_hbm.1, bf16[512,128]{1,0:T(8,128)(2,1)} %g_hbm.1), custom_call_target="tpu_custom_call" | custom-call | tf_op jit(solution)/shard_map/pack/pallas_call | solution.py:335
  8.5 0.0 copy-start
  8.5 19.4 %all-to-all-start = ((bf16[128,24,128]{2,1,0:T(8,128)(2,1)}), bf16[128,24,128]{2,1,0:T(8,128)(2,1)S(1)}, u32[]{:S(2)}, u32[]{:S(2)}) async-start(bf16[128,24,128]{2,1,0:T(8,128)(2,1)} %bitcast), calls=%async_computation | async-start | bytes 1572864 | tf_op jit(solution)/shard_map/all_to_all | solution.py:383
  27.9 0.0 collective-permute-done
  27.9 0.0 copy-done
  27.9 2.8 %collective-permute-start.1 = (s32[2,512]{1,0:T(2,128)S(1)}, s32[2,512]{1,0:T(2,128)S(1)}, u32[]{:S(2)}, u32[]{:S(2)}) collective-permute-start(s32[2,512]{1,0:T(2,128)S(1)} %pad_add_fusion.1), channel_id=1, source_target_pairs={{0,4},{4,0},{8,12},{12,8},{16,20},{20,16},{24,28},{28,24},{32,36},... | collective-permute-start | bytes 12296 | tf_op jit(solution)/shard_map/ppermute | solution.py:390
  30.8 0.8 collective-permute-done.1
  31.6 1.3 %meta.1.rows_ref = s32[8,512]{1,0:T(8,128)S(1)} custom-call(s32[3,512]{1,0:T(4,128)S(1)} %pad_add_fusion.orders_ref, s32[1,512]{1,0:T(1,128)S(1)} %get-tuple-element.6.code_ref), custom_call_target="tpu_custom_call" | custom-call | flops 12000000000 | bytes 32768 | tf_op jit(solution)/shard_map/meta/pallas_call | solution.py:348
  32.8 20.6 %all-to-all-done.arr_ref = bf16[128,24,128]{2,1,0:T(8,128)(2,1)S(1)} async-done(((bf16[128,24,128]{2,1,0:T(8,128)(2,1)}), bf16[128,24,128]{2,1,0:T(8,128)(2,1)S(1)}, u32[]{:S(2)}, u32[]{:S(2)}) %all-to-all-start) | async-done | bytes 786464 | tf_op jit(solution)/shard_map/all_to_all | solution.py:383
  53.4 5.1 %attend.1 = bf16[128,24,128]{2,1,0:T(8,128)(2,1)S(1)} custom-call(bf16[128,24,128]{2,1,0:T(8,128)(2,1)S(1)} %all-to-all-done.arr_ref, s32[8,512]{1,0:T(8,128)S(1)} %meta.1.rows_ref), custom_call_target="tpu_custom_call" | custom-call | tf_op jit(solution)/shard_map/attend/pallas_call | solution.py:361
  58.6 35.9 %all_to_all.10 = bf16[128,24,128]{2,1,0:T(8,128)(2,1)S(1)} all-to-all(bf16[128,24,128]{2,1,0:T(8,128)(2,1)S(1)} %attend.1), channel_id=1, replica_groups=mesh['seq'=128,'head'=4] {'seq'}, dimensions={0} | all-to-all | bytes 1572864 | tf_op jit(solution)/shard_map/all_to_all | solution.py:383
  94.5 1.7 %restore.1 = (bf16[512,128]{1,0:T(8,128)(2,1)}, bf16[512,128]{1,0:T(8,128)(2,1)}, bf16[512,128]{1,0:T(8,128)(2,1)}) custom-call(bf16[64,2,24,128]{3,2,1,0:T(8,128)(2,1)S(1)} %bitcast.2, s32[1,512]{1,0:T(1,128)S(1)} %get-tuple-element.6.code_ref), custom_call_target="tpu_custom_call" | custom-call | tf_op jit(solution)/shard_map/restore/pallas_call | solution.py:374
  (3 shorter events, 0.0 us)
Async XLA Ops:
  0.6 27.3 %collective-permute-start = (s32[1,512]{1,0:T(1,128)}, s32[1,512]{1,0:T(1,128)S(1)}, u32[]{:S(2)}, u32[]{:S(2)}) collective-permute-start(s32[1,512]{1,0:T(1,128)} %param.8), channel_id=1, source_target_pairs={{0,8},{4,12},{8,16},{12,20},{16,24},{20,28},{24,32},{28,36},{32,40... | collective-permute-start | bytes 6152 | tf_op jit(solution)/shard_map/ppermute | solution.py:388
  8.5 19.5 %copy-start = (s32[1,512]{1,0:T(1,128)S(1)}, s32[1,512]{1,0:T(1,128)}, u32[]{:S(2)}) copy-start(s32[1,512]{1,0:T(1,128)} %param.8) | copy-start | bytes 6148
  8.5 45.0 %all-to-all-start = ((bf16[128,24,128]{2,1,0:T(8,128)(2,1)}), bf16[128,24,128]{2,1,0:T(8,128)(2,1)S(1)}, u32[]{:S(2)}, u32[]{:S(2)}) async-start(bf16[128,24,128]{2,1,0:T(8,128)(2,1)} %bitcast), calls=%async_computation | async-start | bytes 1572864 | tf_op jit(solution)/shard_map/all_to_all | solution.py:383
  27.9 3.6 %collective-permute-start.1 = (s32[2,512]{1,0:T(2,128)S(1)}, s32[2,512]{1,0:T(2,128)S(1)}, u32[]{:S(2)}, u32[]{:S(2)}) collective-permute-start(s32[2,512]{1,0:T(2,128)S(1)} %pad_add_fusion.1), channel_id=1, source_target_pairs={{0,4},{4,0},{8,12},{12,8},{16,20},{20,16},{24,28},{28,24},{32,36},... | collective-permute-start | bytes 12296 | tf_op jit(solution)/shard_map/ppermute | solution.py:390

commit v7 on v6

--- a/solution.py
+++ b/solution.py
@@ -204,26 +204,30 @@
     def item(prior, own, grads, prior_pos, own_pos):
         q = own["qb"]
         pos = jnp.concatenate([column(own_pos)] * (n // 128), axis=1)
-        s0 = tn(q, prior["qb"]) * prior["scale"]
-        s0 = jnp.where(prior_pos.astype(F32) < pos, s0, masked_score)
-        s1 = tn(q, own["qb"][:, first]) * own["scale"][:, first]
+
+        def most(name):
+            return jnp.concatenate([prior[name], own[name][:, first]], axis=1)
+
+        v1, v2 = most("vb"), own["vb"][:, last]
+        s1 = tn(q, most("qb")) * most("scale")
         s2 = tn(q[:, last], own["qb"][:, last]) * own["scale"][:, last]
         yield
 
         def triangle(s):
             return jnp.where(col < row, s, jnp.where(col == row, self_score, masked_score))
 
-        s1 = jnp.concatenate([triangle(s1[:half]), s1[half:]], axis=0)
+        s0 = jnp.where(prior_pos.astype(F32) < pos, s1[:, :n], masked_score)
+        s1 = jnp.concatenate([triangle(s1[:half, n:]), s1[half:, n:]], axis=0)
         s2 = triangle(s2)
         top0, top1, top2 = (jnp.max(s, axis=1, keepdims=True) for s in (s0, s1, s2))
         top_low, top_high = low_high(jnp.maximum(top0, top1))
         top_high = jnp.maximum(top_high, top2)
         top = jnp.concatenate([top_low, top_high], axis=0)
-        p0, p1, p2 = jnp.exp2(s0 - top), jnp.exp2(s1 - top), jnp.exp2(s2 - top_high)
-        b0, b1, b2 = p0.astype(BF16), p1.astype(BF16), p2.astype(BF16)
+        p1 = jnp.concatenate([jnp.exp2(s0 - top), jnp.exp2(s1 - top)], axis=1)
+        p2 = jnp.exp2(s2 - top_high)
+        b1, b2 = p1.astype(BF16), p2.astype(BF16)
         yield
-        v0, v1, v2 = prior["vb"], own["vb"][:, first], own["vb"][:, last]
-        summed = late(nt(v0, b0) + nt(v1, b1), nt(v2, b2))
+        summed = late(nt(v1, b1), nt(v2, b2))
         inverse = 1.0 / summed[h : h + 1]
         out = (summed[:h] * inverse).astype(BF16)
         grad = (grads * inverse).astype(BF16)
@@ -231,18 +235,13 @@
         terms = [x.astype(F32) for x in (grad, *two_terms(-delta))]
         left = jnp.concatenate([*terms, pad], axis=0).astype(BF16)
         yield
-        d0 = (p0 * tn(left, v0)).astype(BF16)
         d1 = (p1 * tn(left, v1)).astype(BF16)
         d2 = (p2 * tn(left[:, last], v2)).astype(BF16)
         yield
-        dq = late(
-            nt(prior["key"], d0) + nt(own["key"][:, first], d1), nt(own["key"][:, last], d2)
-        )
-        sums_prior = (mm(q, d0), mm(grad, b0))
-        sums_own = tuple(
-            jnp.concatenate([mm(x, lo), mm(x[:, last], hi)], axis=1)
-            for x, lo, hi in ((q, d1, d2), (grad, b1, b2))
-        )
+        dq = late(nt(most("key"), d1), nt(own["key"][:, last], d2))
+        sums = [(mm(x, lo), mm(x[:, last], hi)) for x, lo, hi in ((q, d1, d2), (grad, b1, b2))]
+        sums_prior = tuple(lo[:, :n] for lo, _ in sums)
+        sums_own = tuple(jnp.concatenate([lo[:, n:], hi], axis=1) for lo, hi in sums)
         yield out, dq, sums_prior, sums_own
 
     pos_z, pos_a, pos_b = rows_ref[0:1], rows_ref[1:2], rows_ref[2:3]

time: 96.4 us -> 96.3 us (level)
  no operation moved by 1% of the time
where the time goes in v7:
time: 96.3 us; the launch traced here: 96 us
  blocking collectives  35.9 us (37%)
  starting transfers between devices  27.1 us (28%)
  waiting for transfers between devices  21.4 us (22%)
  Pallas kernels  10.9 us (11%)
    all_to_all x1, blocking collectives, exchange(): lax.all_to_all(message, 'seq', split_axis=0, concat_axis=0, tiled=True)  35.9 us
    all_to_all x1, waiting for transfers between devices, exchange(): lax.all_to_all(message, 'seq', split_axis=0, concat_axis=0, tiled=True)  20.6 us
    all_to_all x1, starting transfers between devices, exchange(): lax.all_to_all(message, 'seq', split_axis=0, concat_axis=0, tiled=True)  19.4 us
    pallas_call x1, Pallas kernels, attend(): pl.pallas_call(attend_kernel, out_shape=struct(shape, BF16), scratch_shap...  5.02 us
    ppermute x1, starting transfers between devices, per_device(): lax.ppermute(bucket_order, 'seq', [(i, (i + 2) % PEERS) for i in peers])  4.83 us
    pallas_call x1, Pallas kernels, pack(): pl.pallas_call(pack_kernel, in_specs=[pl.BlockSpec(memory_space=pltpu.HBM...  2.97 us
    ppermute x1, starting transfers between devices, per_device(): other = lax.ppermute(held, 'seq', [(i, i ^ 1) for i in peers])  2.8 us
  transfers between devices with their start and end apart: 3, of which 2 were waited for; matrix products, arithmetic and copies ran while one was open for 0% of the time, Pallas kernels for 4%

profile of v7, /device:TPU:1, one launch (start us, length us, event | category | flops | bytes accessed | tf_op | source)
XLA Modules:
  0.0 96.0 jit_solution(7500608466978507692)
XLA Ops:
  0.6 4.8 %collective-permute-start = (s32[1,512]{1,0:T(1,128)}, s32[1,512]{1,0:T(1,128)S(1)}, u32[]{:S(2)}, u32[]{:S(2)}) collective-permute-start(s32[1,512]{1,0:T(1,128)} %param.8), channel_id=1, source_target_pairs={{0,8},{4,12},{8,16},{12,20},{16,24},{20,28},{24,32},{28,36},{32,40... | collective-permute-start | bytes 6152 | tf_op jit(solution)/shard_map/ppermute | solution.py:387
  5.5 3.0 %pack.1 = (bf16[64,2,24,128]{3,2,1,0:T(8,128)(2,1)}, s32[1,512]{1,0:T(1,128)S(1)}) custom-call(s32[1,512]{1,0:T(1,128)} %slot_hbm.1, bf16[512,128]{1,0:T(8,128)(2,1)} %q_hbm.1, bf16[512,128]{1,0:T(8,128)(2,1)} %v_hbm.1, bf16[512,128]{1,0:T(8,128)(2,1)} %g_hbm.1), custom_call_target="tpu_custom_call" | custom-call | tf_op jit(solution)/shard_map/pack/pallas_call | solution.py:334
  8.5 0.0 copy-start
  8.5 19.4 %all-to-all-start = ((bf16[128,24,128]{2,1,0:T(8,128)(2,1)}), bf16[128,24,128]{2,1,0:T(8,128)(2,1)S(1)}, u32[]{:S(2)}, u32[]{:S(2)}) async-start(bf16[128,24,128]{2,1,0:T(8,128)(2,1)} %bitcast), calls=%async_computation | async-start | bytes 1572864 | tf_op jit(solution)/shard_map/all_to_all | solution.py:382
  27.9 0.0 collective-permute-done
  27.9 0.0 copy-done
  27.9 2.8 %collective-permute-start.1 = (s32[2,512]{1,0:T(2,128)S(1)}, s32[2,512]{1,0:T(2,128)S(1)}, u32[]{:S(2)}, u32[]{:S(2)}) collective-permute-start(s32[2,512]{1,0:T(2,128)S(1)} %pad_add_fusion.1), channel_id=1, source_target_pairs={{0,4},{4,0},{8,12},{12,8},{16,20},{20,16},{24,28},{28,24},{32,36},... | collective-permute-start | bytes 12296 | tf_op jit(solution)/shard_map/ppermute | solution.py:389
  30.8 0.8 collective-permute-done.1
  31.6 1.3 %meta.1.rows_ref = s32[8,512]{1,0:T(8,128)S(1)} custom-call(s32[3,512]{1,0:T(4,128)S(1)} %pad_add_fusion.orders_ref, s32[1,512]{1,0:T(1,128)S(1)} %get-tuple-element.6.code_ref), custom_call_target="tpu_custom_call" | custom-call | flops 12000000000 | bytes 32768 | tf_op jit(solution)/shard_map/meta/pallas_call | solution.py:347
  32.8 20.6 %all-to-all-done.arr_ref = bf16[128,24,128]{2,1,0:T(8,128)(2,1)S(1)} async-done(((bf16[128,24,128]{2,1,0:T(8,128)(2,1)}), bf16[128,24,128]{2,1,0:T(8,128)(2,1)S(1)}, u32[]{:S(2)}, u32[]{:S(2)}) %all-to-all-start) | async-done | bytes 786464 | tf_op jit(solution)/shard_map/all_to_all | solution.py:382
  53.4 5.0 %attend.1 = bf16[128,24,128]{2,1,0:T(8,128)(2,1)S(1)} custom-call(bf16[128,24,128]{2,1,0:T(8,128)(2,1)S(1)} %all-to-all-done.arr_ref, s32[8,512]{1,0:T(8,128)S(1)} %meta.1.rows_ref), custom_call_target="tpu_custom_call" | custom-call | tf_op jit(solution)/shard_map/attend/pallas_call | solution.py:360
  58.5 35.9 %all_to_all.10 = bf16[128,24,128]{2,1,0:T(8,128)(2,1)S(1)} all-to-all(bf16[128,24,128]{2,1,0:T(8,128)(2,1)S(1)} %attend.1), channel_id=1, replica_groups=mesh['seq'=128,'head'=4] {'seq'}, dimensions={0} | all-to-all | bytes 1572864 | tf_op jit(solution)/shard_map/all_to_all | solution.py:382
  94.3 1.7 %restore.1 = (bf16[512,128]{1,0:T(8,128)(2,1)}, bf16[512,128]{1,0:T(8,128)(2,1)}, bf16[512,128]{1,0:T(8,128)(2,1)}) custom-call(bf16[64,2,24,128]{3,2,1,0:T(8,128)(2,1)S(1)} %bitcast.2, s32[1,512]{1,0:T(1,128)S(1)} %get-tuple-element.6.code_ref), custom_call_target="tpu_custom_call" | custom-call | tf_op jit(solution)/shard_map/restore/pallas_call | solution.py:373
  (3 shorter events, 0.0 us)
Async XLA Ops:
  0.6 27.3 %collective-permute-start = (s32[1,512]{1,0:T(1,128)}, s32[1,512]{1,0:T(1,128)S(1)}, u32[]{:S(2)}, u32[]{:S(2)}) collective-permute-start(s32[1,512]{1,0:T(1,128)} %param.8), channel_id=1, source_target_pairs={{0,8},{4,12},{8,16},{12,20},{16,24},{20,28},{24,32},{28,36},{32,40... | collective-permute-start | bytes 6152 | tf_op jit(solution)/shard_map/ppermute | solution.py:387
  8.5 19.5 %copy-start = (s32[1,512]{1,0:T(1,128)S(1)}, s32[1,512]{1,0:T(1,128)}, u32[]{:S(2)}) copy-start(s32[1,512]{1,0:T(1,128)} %param.8) | copy-start | bytes 6148
  8.5 45.0 %all-to-all-start = ((bf16[128,24,128]{2,1,0:T(8,128)(2,1)}), bf16[128,24,128]{2,1,0:T(8,128)(2,1)S(1)}, u32[]{:S(2)}, u32[]{:S(2)}) async-start(bf16[128,24,128]{2,1,0:T(8,128)(2,1)} %bitcast), calls=%async_computation | async-start | bytes 1572864 | tf_op jit(solution)/shard_map/all_to_all | solution.py:382
  27.9 3.6 %collective-permute-start.1 = (s32[2,512]{1,0:T(2,128)S(1)}, s32[2,512]{1,0:T(2,128)S(1)}, u32[]{:S(2)}, u32[]{:S(2)}) collective-permute-start(s32[2,512]{1,0:T(2,128)S(1)} %pad_add_fusion.1), channel_id=1, source_target_pairs={{0,4},{4,0},{8,12},{12,8},{16,20},{20,16},{24,28},{28,24},{32,36},... | collective-permute-start | bytes 12296 | tf_op jit(solution)/shard_map/ppermute | solution.py:389

commit v8 on v6

--- a/solution.py
+++ b/solution.py
@@ -74,8 +74,8 @@
             [(slot_hbm, slot_ref), (q_hbm, q_ref), (v_hbm, v_ref), (g_hbm, g_ref)]
         )
     ]
-    for copy in copies:
-        copy.start()
+    for i, copy in enumerate(copies):
+        copy.start(priority=int(i == 0))
     copies[0].wait()
     block = slot_ref[...] >> 9
     local = block.shape[1]

time: 96.4 us -> 96.4 us (level)
  no operation moved by 1% of the time
where the time goes in v8:
time: 96.4 us; the launch traced here: 96.1 us
  blocking collectives  35.9 us (37%)
  starting transfers between devices  27.1 us (28%)
  waiting for transfers between devices  21.4 us (22%)
  Pallas kernels  11.1 us (12%)
    all_to_all x1, blocking collectives, exchange(): lax.all_to_all(message, 'seq', split_axis=0, concat_axis=0, tiled=True)  35.9 us
    all_to_all x1, waiting for transfers between devices, exchange(): lax.all_to_all(message, 'seq', split_axis=0, concat_axis=0, tiled=True)  20.6 us
    all_to_all x1, starting transfers between devices, exchange(): lax.all_to_all(message, 'seq', split_axis=0, concat_axis=0, tiled=True)  19.4 us
    pallas_call x1, Pallas kernels, attend(): pl.pallas_call(attend_kernel, out_shape=struct(shape, BF16), scratch_shap...  5.14 us
    ppermute x1, starting transfers between devices, per_device(): lax.ppermute(bucket_order, 'seq', [(i, (i + 2) % PEERS) for i in peers])  4.83 us
    pallas_call x1, Pallas kernels, pack(): pl.pallas_call(pack_kernel, in_specs=[pl.BlockSpec(memory_space=pltpu.HBM...  2.97 us
    ppermute x1, starting transfers between devices, per_device(): other = lax.ppermute(held, 'seq', [(i, i ^ 1) for i in peers])  2.8 us
  transfers between devices with their start and end apart: 3, of which 2 were waited for; matrix products, arithmetic and copies ran while one was open for 0% of the time, Pallas kernels for 4%

profile of v8, /device:TPU:1, one launch (start us, length us, event | category | flops | bytes accessed | tf_op | source)
XLA Modules:
  0.0 96.1 jit_solution(3082940430735249120)
XLA Ops:
  0.6 4.8 %collective-permute-start = (s32[1,512]{1,0:T(1,128)}, s32[1,512]{1,0:T(1,128)S(1)}, u32[]{:S(2)}, u32[]{:S(2)}) collective-permute-start(s32[1,512]{1,0:T(1,128)} %param.8), channel_id=1, source_target_pairs={{0,8},{4,12},{8,16},{12,20},{16,24},{20,28},{24,32},{28,36},{32,40... | collective-permute-start | bytes 6152 | tf_op jit(solution)/shard_map/ppermute | solution.py:388
  5.5 3.0 %pack.1 = (bf16[64,2,24,128]{3,2,1,0:T(8,128)(2,1)}, s32[1,512]{1,0:T(1,128)S(1)}) custom-call(s32[1,512]{1,0:T(1,128)} %slot_hbm.1, bf16[512,128]{1,0:T(8,128)(2,1)} %q_hbm.1, bf16[512,128]{1,0:T(8,128)(2,1)} %v_hbm.1, bf16[512,128]{1,0:T(8,128)(2,1)} %g_hbm.1), custom_call_target="tpu_custom_call" | custom-call | tf_op jit(solution)/shard_map/pack/pallas_call | solution.py:335
  8.5 0.0 copy-start
  8.5 19.4 %all-to-all-start = ((bf16[128,24,128]{2,1,0:T(8,128)(2,1)}), bf16[128,24,128]{2,1,0:T(8,128)(2,1)S(1)}, u32[]{:S(2)}, u32[]{:S(2)}) async-start(bf16[128,24,128]{2,1,0:T(8,128)(2,1)} %bitcast), calls=%async_computation | async-start | bytes 1572864 | tf_op jit(solution)/shard_map/all_to_all | solution.py:383
  27.9 0.0 collective-permute-done
  27.9 0.0 copy-done
  27.9 2.8 %collective-permute-start.1 = (s32[2,512]{1,0:T(2,128)S(1)}, s32[2,512]{1,0:T(2,128)S(1)}, u32[]{:S(2)}, u32[]{:S(2)}) collective-permute-start(s32[2,512]{1,0:T(2,128)S(1)} %pad_add_fusion.1), channel_id=1, source_target_pairs={{0,4},{4,0},{8,12},{12,8},{16,20},{20,16},{24,28},{28,24},{32,36},... | collective-permute-start | bytes 12296 | tf_op jit(solution)/shard_map/ppermute | solution.py:390
  30.8 0.8 collective-permute-done.1
  31.6 1.3 %meta.1.rows_ref = s32[8,512]{1,0:T(8,128)S(1)} custom-call(s32[3,512]{1,0:T(4,128)S(1)} %pad_add_fusion.orders_ref, s32[1,512]{1,0:T(1,128)S(1)} %get-tuple-element.6.code_ref), custom_call_target="tpu_custom_call" | custom-call | flops 12000000000 | bytes 32768 | tf_op jit(solution)/shard_map/meta/pallas_call | solution.py:348
  32.8 20.6 %all-to-all-done.arr_ref = bf16[128,24,128]{2,1,0:T(8,128)(2,1)S(1)} async-done(((bf16[128,24,128]{2,1,0:T(8,128)(2,1)}), bf16[128,24,128]{2,1,0:T(8,128)(2,1)S(1)}, u32[]{:S(2)}, u32[]{:S(2)}) %all-to-all-start) | async-done | bytes 786464 | tf_op jit(solution)/shard_map/all_to_all | solution.py:383
  53.4 5.1 %attend.1 = bf16[128,24,128]{2,1,0:T(8,128)(2,1)S(1)} custom-call(bf16[128,24,128]{2,1,0:T(8,128)(2,1)S(1)} %all-to-all-done.arr_ref, s32[8,512]{1,0:T(8,128)S(1)} %meta.1.rows_ref), custom_call_target="tpu_custom_call" | custom-call | tf_op jit(solution)/shard_map/attend/pallas_call | solution.py:361
  58.6 35.9 %all_to_all.10 = bf16[128,24,128]{2,1,0:T(8,128)(2,1)S(1)} all-to-all(bf16[128,24,128]{2,1,0:T(8,128)(2,1)S(1)} %attend.1), channel_id=1, replica_groups=mesh['seq'=128,'head'=4] {'seq'}, dimensions={0} | all-to-all | bytes 1572864 | tf_op jit(solution)/shard_map/all_to_all | solution.py:383
  94.5 1.7 %restore.1 = (bf16[512,128]{1,0:T(8,128)(2,1)}, bf16[512,128]{1,0:T(8,128)(2,1)}, bf16[512,128]{1,0:T(8,128)(2,1)}) custom-call(bf16[64,2,24,128]{3,2,1,0:T(8,128)(2,1)S(1)} %bitcast.2, s32[1,512]{1,0:T(1,128)S(1)} %get-tuple-element.6.code_ref), custom_call_target="tpu_custom_call" | custom-call | tf_op jit(solution)/shard_map/restore/pallas_call | solution.py:374
  (3 shorter events, 0.0 us)
Async XLA Ops:
  0.6 27.3 %collective-permute-start = (s32[1,512]{1,0:T(1,128)}, s32[1,512]{1,0:T(1,128)S(1)}, u32[]{:S(2)}, u32[]{:S(2)}) collective-permute-start(s32[1,512]{1,0:T(1,128)} %param.8), channel_id=1, source_target_pairs={{0,8},{4,12},{8,16},{12,20},{16,24},{20,28},{24,32},{28,36},{32,40... | collective-permute-start | bytes 6152 | tf_op jit(solution)/shard_map/ppermute | solution.py:388
  8.5 19.5 %copy-start = (s32[1,512]{1,0:T(1,128)S(1)}, s32[1,512]{1,0:T(1,128)}, u32[]{:S(2)}) copy-start(s32[1,512]{1,0:T(1,128)} %param.8) | copy-start | bytes 6148
  8.5 45.0 %all-to-all-start = ((bf16[128,24,128]{2,1,0:T(8,128)(2,1)}), bf16[128,24,128]{2,1,0:T(8,128)(2,1)S(1)}, u32[]{:S(2)}, u32[]{:S(2)}) async-start(bf16[128,24,128]{2,1,0:T(8,128)(2,1)} %bitcast), calls=%async_computation | async-start | bytes 1572864 | tf_op jit(solution)/shard_map/all_to_all | solution.py:383
  27.9 3.6 %collective-permute-start.1 = (s32[2,512]{1,0:T(2,128)S(1)}, s32[2,512]{1,0:T(2,128)S(1)}, u32[]{:S(2)}, u32[]{:S(2)}) collective-permute-start(s32[2,512]{1,0:T(2,128)S(1)} %pad_add_fusion.1), channel_id=1, source_target_pairs={{0,4},{4,0},{8,12},{12,8},{16,20},{20,16},{24,28},{28,24},{32,36},... | collective-permute-start | bytes 12296 | tf_op jit(solution)/shard_map/ppermute | solution.py:390
